TPU v7x, 32 devices: a whole 2x2x4 slice. The times are simulated.
32 devices in a mesh: grp: 2 (over y), row: 4 (over z), col: 2 (over x), pair: 2 (over core).
Axes of the slice: x: 2, y: 2, z: 4, core: 2. Of those that a mesh axis runs over, the one named last changes fastest.
Arguments:
- features_in: bfloat16 [128, 32, 512], P('grp', 'row', ('col', 'pair')), parts along dimension 0, may hold values from -8 to 8
- filters_one: bfloat16 [64, 3, 3, 64], replicated, may hold values from -0.25 to 0.25
- filters_two: bfloat16 [512, 3, 3, 256], P('row'), may hold values from -0.125 to 0.125
- out_grad: bfloat16 [1024, 128, 8], P(('grp', 'row'), ('col', 'pair')), parts along dimension 0, may hold values from -24 to 24
Outputs:
- input_grad: bfloat16 [128, 32, 512], P('grp', 'row', ('col', 'pair')), parts along dimension 0
- grad_one: float32 [128, 3, 3, 64], P('grp'), parts along dimension 0
- grad_two: float32 [1024, 3, 3, 256], P(('grp', 'row')), parts along dimension 0
There are 2 independent parts, one for each index of `grp`. A program takes and returns all parts, laid end to end along the dimension named above; an argument that names none is the same for every part. Nothing has to cross between parts.
All inputs are finite; a program needn't handle non-finite values.
Results may differ from a plain program's by a relative error of at most 0.015.
Values may be sent and summed in bfloat16 or wider, within the bound.
A program may use at most 64 MiB of HBM per device.

v0:
```python
import math

import jax
import jax.numpy as jnp
from jax import lax
from jax.sharding import PartitionSpec as P


def padded_2(cells, sides, width):
    for axis, dim in sides:
        count = lax.axis_size(axis)
        ends = count - 1
        head = lax.slice_in_dim(cells, 0, width, axis=dim)
        tail = lax.slice_in_dim(cells, cells.shape[dim] - width, cells.shape[dim], axis=dim)
        cells = jnp.concatenate(
            [
                lax.ppermute(tail, axis, [(i, (i + 1) % count) for i in range(ends)]),
                cells,
                lax.ppermute(head, axis, [((i + 1) % count, i) for i in range(ends)]),
            ],
            axis=dim,
        )
    return cells


def conv_valid(padded, kernel):
    return lax.conv_general_dilated(
        padded[None],
        kernel,
        (1, 1),
        "VALID",
        dimension_numbers=("NCHW", "OHWI", "NCHW"),
        preferred_element_type=jnp.float32,
    )[0]


def flip_kernel(kernel):
    return jnp.transpose(kernel[:, ::-1, ::-1, :], (3, 1, 2, 0))


def silu_slope(values):
    sigmoid_value = jax.nn.sigmoid(values)
    return sigmoid_value * (1.0 + values * (1.0 - sigmoid_value))


def tap_grads(gradient, padded):
    row_count, col_count = (gradient.shape[1], gradient.shape[2])
    tap_list = []
    for first_tap in range(3):
        tap_row = []
        for second_tap in range(3):
            window = padded[
                :, first_tap : first_tap + row_count, second_tap : second_tap + col_count
            ]
            tap_row.append(
                jnp.einsum("ohw,chw->oc", gradient, window, preferred_element_type=jnp.float32)
            )
        tap_list.append(jnp.stack(tap_row, 1))
    return jnp.stack(tap_list, 1)


def pool_columns(active):
    channels, row_count, col_count = active.shape
    folded = active.reshape(channels, row_count // 4, 2, 2, col_count // 4, 2, 2).mean(axis=(3, 6))
    return jnp.transpose(folded, (0, 2, 4, 3, 1)).reshape(
        channels * 4, col_count // 4, row_count // 4
    )


def unpool_columns(gradient):
    quad_count, col_count, row_count = gradient.shape
    ordered = jnp.transpose(
        gradient.reshape(quad_count // 4, 2, 2, col_count, row_count), (0, 4, 1, 3, 2)
    )
    spread = (
        jnp.broadcast_to(
            ordered[:, :, :, None, :, :, None], (quad_count // 4, row_count, 2, 2, col_count, 2, 2)
        )
        * 0.25
    )
    return spread.reshape(quad_count // 4, row_count * 4, col_count * 4)


def local(features_in, filters_one, filters_two, out_grad):
    band_rows = features_in.shape[1]
    strip_cols = features_in.shape[2]
    height = band_rows * lax.axis_size("row")
    width = strip_cols * lax.axis_size(("col", "pair"))
    padded_in = padded_2(features_in, (("row", 1), (("col", "pair"), 2)), 1)
    pre_one = conv_valid(padded_in, filters_one)
    pooled = pool_columns(jax.nn.silu(pre_one)).astype(jnp.bfloat16)
    with_edges = padded_2(pooled, ((("col", "pair"), 1),), 1)
    column_strip = lax.all_gather(with_edges, "row", axis=2, tiled=True)
    strip_padded = jnp.pad(column_strip, ((0, 0), (0, 0), (1, 1)))
    swapped = jnp.transpose(filters_two, (0, 2, 1, 3))
    pre_two = conv_valid(strip_padded, swapped)
    grad_pre_two = (out_grad.astype(jnp.float32) * silu_slope(pre_two)).astype(jnp.bfloat16)
    pooled_height = column_strip.shape[2]
    pooled_width = strip_cols // 4 * lax.axis_size(("col", "pair"))
    local_two = jnp.transpose(tap_grads(grad_pre_two, strip_padded), (0, 2, 1, 3))
    grad_two = lax.psum(local_two, ("col", "pair")) / math.sqrt(pooled_height * pooled_width)
    padded_grad = jnp.pad(grad_pre_two, ((0, 0), (2, 2), (1, 1)))
    spread_grad = conv_valid(padded_grad, flip_kernel(swapped))
    with_ghosts = padded_2(spread_grad, ((("col", "pair"), 1),), 1)
    real_columns = spread_grad[:, 1:-1, :]
    real_columns = real_columns.at[:, 0, :].add(with_ghosts[:, 0, :])
    real_columns = real_columns.at[:, -1, :].add(with_ghosts[:, -1, :])
    grad_pooled = lax.psum_scatter(real_columns, "row", scatter_dimension=2, tiled=True)
    grad_pre_one = (unpool_columns(grad_pooled) * silu_slope(pre_one)).astype(jnp.bfloat16)
    local_one = tap_grads(grad_pre_one, padded_in)
    grad_one = lax.psum(local_one, ("row", "col", "pair")) / math.sqrt(height * width)
    rimmed_one = padded_2(grad_pre_one, (("row", 1), (("col", "pair"), 2)), 1)
    input_grad = conv_valid(rimmed_one, flip_kernel(filters_one)).astype(jnp.bfloat16)
    return (input_grad, grad_one, grad_two)


def solution(mesh):
    in_specs = (
        P("grp", "row", ("col", "pair")),
        P(),
        P("row", None, None, None),
        P(("grp", "row"), ("col", "pair"), None),
    )
    out_specs = (
        P("grp", "row", ("col", "pair")),
        P("grp", None, None, None),
        P(("grp", "row"), None, None, None),
    )
    return jax.shard_map(local, mesh=mesh, in_specs=in_specs, out_specs=out_specs, check_vma=False)
```

profile of v0, /device:TPU:0, one launch (start us, length us, event | category | flops | bytes accessed | tf_op | source)
XLA Modules:
  0.0 211.8 jit_solution(14888131075437018906)
XLA Ops:
  8.1 1.0 copy.216
  9.1 4.9 %collective-permute-start = (bf16[64,1,128]{2,0,1:T(8,128)(2,1)S(1)}, bf16[64,1,128]{2,0,1:T(8,128)(2,1)S(1)}, u32[]{:S(2)}, u32[]{:S(2)}) collective-permute-start(bf16[64,1,128]{2,0,1:T(8,128)(2,1)S(1)} %get-tuple-element.58), channel_id=1, source_target_pairs={{0,4},{4,8},{8,12},{1,5},{5,9},{9,13},{2,6},{6,10},{10,14},{3,7},{... | collective-permute-start | bytes 49160 | tf_op jit(solution)/shard_map/ppermute | solution.py:17
  14.0 1.3 collective-permute-start.1
  15.4 0.9 constant_dynamic-update-slice_fusion.1
  16.4 3.3 %collective-permute-done.1 = bf16[64,1,128]{2,0,1:T(8,128)(2,1)S(1)} collective-permute-done((bf16[64,1,128]{2,0,1:T(8,128)(2,1)S(1)}, bf16[64,1,128]{2,0,1:T(8,128)(2,1)S(1)}, u32[]{:S(2)}, u32[]{:S(2)}) %collective-permute-start.1) | collective-permute-done | bytes 16416 | tf_op jit(solution)/shard_map/ppermute | solution.py:19
  19.7 1.3 collective-permute-start.3
  21.0 3.0 %collective-permute-start.2 = (bf16[64,10,1]{2,0,1:T(8,128)(2,1)S(1)}, bf16[64,10,1]{2,0,1:T(8,128)(2,1)S(1)}, u32[]{:S(2)}, u32[]{:S(2)}) collective-permute-start(bf16[64,10,1]{2,0,1:T(8,128)(2,1)S(1)} %get-tuple-element.51), channel_id=1, source_target_pairs={{0,1},{1,2},{2,3},{4,5},{5,6},{6,7},{8,9},{9,10},{10,11},{12,13},{... | collective-permute-start | bytes 3848 | tf_op jit(solution)/shard_map/ppermute | solution.py:17
  24.1 1.0 collective-permute-done.2
  25.1 0.2 maximum_bitcast_fusion.4
  25.3 0.3 copy.265
  25.9 0.6 copy-done.3
  26.5 0.8 convolution_select_fusion.1
  27.6 0.9 fusion.3
  28.8 1.3 collective-permute-start.5
  30.1 4.9 %collective-permute-start.4 = (bf16[256,1,2]{1,0,2:T(8,128)(2,1)S(1)}, bf16[256,1,2]{1,0,2:T(8,128)(2,1)S(1)}, u32[]{:S(2)}, u32[]{:S(2)}) collective-permute-start(bf16[256,1,2]{1,0,2:T(8,128)(2,1)S(1)} %get-tuple-element.55), channel_id=1, source_target_pairs={{0,1},{1,2},{2,3},{4,5},{5,6},{6,7},{8,9},{9,10},{10,11},{12,13},{... | collective-permute-start | bytes 3080 | tf_op jit(solution)/shard_map/ppermute | solution.py:17
  35.0 0.2 copy.264
  35.3 0.7 collective-permute-done.4
  36.0 0.1 pad_maximum_fusion.9
  36.2 13.7 %all_gather.3 = bf16[256,34,8]{0,1,2:T(8,128)(2,1)S(1)} all-gather(bf16[256,34,2]{0,1,2:T(8,128)(2,1)S(1)} %copy.226), channel_id=1, replica_groups=mesh['grp'=2,'row'=4,'col'=2,'pair'=2] {'row'}, dimensions={2}, use_global_device_ids=true | all-gather | bytes 174080 | tf_op jit(solution)/shard_map/all_gather | solution.py:93
  50.1 1.0 fusion.6
  51.3 0.2 convolution_bitcast_fusion
  51.5 0.2 convolution_bitcast_fusion.1
  51.7 0.2 convolution_bitcast_fusion.2
  51.9 0.2 convolution_bitcast_fusion.6
  52.1 0.2 convolution_bitcast_fusion.7
  52.4 0.2 convolution_bitcast_fusion.8
  52.6 0.2 convolution_bitcast_fusion.3
  52.8 1.0 fusion.4
  53.9 2.4 %collective-permute-start.6 = (f32[256,1,8]{0,2,1:T(8,128)S(1)}, f32[256,1,8]{0,2,1:T(8,128)S(1)}, u32[]{:S(2)}, u32[]{:S(2)}) collective-permute-start(f32[256,1,8]{0,2,1:T(8,128)S(1)} %get-tuple-element.48), channel_id=1, source_target_pairs={{0,1},{1,2},{2,3},{4,5},{5,6},{6,7},{8,9},{9,10},{10,11},{12,13},{... | collective-permute-start | bytes 24584 | tf_op jit(solution)/shard_map/ppermute | solution.py:17
  56.3 0.2 convolution_bitcast_fusion.5
  56.6 1.3 collective-permute-start.7
  57.9 6.6 %collective-permute-done.7 = f32[256,1,8]{0,2,1:T(8,128)S(1)} collective-permute-done((f32[256,1,8]{0,2,1:T(8,128)S(1)}, f32[256,1,8]{0,2,1:T(8,128)S(1)}, u32[]{:S(2)}, u32[]{:S(2)}) %collective-permute-start.7) | collective-permute-done | bytes 8224 | tf_op jit(solution)/shard_map/ppermute | solution.py:19
  64.4 0.8 copy.233
  65.3 0.2 convolution_bitcast_fusion.4
  65.7 1.1 maximum_bitcast_fusion
  66.8 18.7 %reduce-scatter.2.cloned.1.call-done = f32[256,32,2]{0,1,2:T(8,128)} async-done(((f32[256,32,8]{0,1,2:T(8,128)}), f32[256,32,2]{0,1,2:T(8,128)}) %reduce-scatter.2.cloned.1.call-update) | async-done | bytes 65552 | tf_op jit(solution)/shard_map/reduce_scatter | solution.py:108
  85.5 0.8 broadcast_multiply_fusion.2
  86.8 0.2 copy.236
  87.1 0.4 copy-done.1
  87.5 0.2 convolution_bitcast_fusion.13
  87.7 1.3 collective-permute-start.8
  89.0 1.3 collective-permute-start.9
  90.3 0.3 convolution_bitcast_fusion.15
  90.6 0.2 convolution_bitcast_fusion.16
  90.8 0.3 convolution_bitcast_fusion.17
  91.0 0.3 convolution_bitcast_fusion.12
  91.3 0.3 convolution_bitcast_fusion.14
  91.6 0.3 convolution_bitcast_fusion.9
  91.9 0.2 convolution_bitcast_fusion.10
  92.0 0.2 convolution_bitcast_fusion.11
  92.4 2.4 %collective-permute-done.9 = bf16[64,1,128]{2,1,0:T(2,128)(2,1)S(1)} collective-permute-done((bf16[64,1,128]{2,1,0:T(2,128)(2,1)S(1)}, bf16[64,1,128]{2,1,0:T(2,128)(2,1)S(1)}, u32[]{:S(2)}, u32[]{:S(2)}) %collective-permute-start.9) | collective-permute-done | bytes 16416 | tf_op jit(solution)/shard_map/ppermute | solution.py:19
  94.9 1.3 collective-permute-start.11
  96.2 3.0 %collective-permute-start.10 = (bf16[64,10,1]{2,0,1:T(8,128)(2,1)S(1)}, bf16[64,10,1]{2,0,1:T(8,128)(2,1)S(1)}, u32[]{:S(2)}, u32[]{:S(2)}) collective-permute-start(bf16[64,10,1]{2,0,1:T(8,128)(2,1)S(1)} %get-tuple-element.49), channel_id=1, source_target_pairs={{0,1},{1,2},{2,3},{4,5},{5,6},{6,7},{8,9},{9,10},{10,11},{12,13},{... | collective-permute-start | bytes 3848 | tf_op jit(solution)/shard_map/ppermute | solution.py:17
  99.3 0.7 pad_maximum_fusion
  100.0 0.2 collective-permute-done.10
  100.3 0.2 maximum_bitcast_fusion.5
  100.5 0.3 copy.266
  101.0 0.6 fusion
  101.7 0.9 copy.259
  102.6 5.7 %all-reduce.7.cloned.1.call-done = f32[128,3,3,256]{3,0,1,2:T(8,128)} async-done(((f32[128,3,3,256]{3,0,1,2:T(8,128)}), f32[128,3,3,256]{3,0,1,2:T(8,128)}) %all-reduce.7.cloned.1.call-update) | async-done | bytes 1179664 | tf_op jit(solution)/shard_map/psum | solution.py:101
  108.3 1.4 broadcast_multiply_fusion
  109.7 1.1 copy.260
  110.8 91.9 %all-reduce.5.cloned.1.call-done = f32[64,3,3,64]{3,0,2,1:T(8,128)} async-done(((f32[64,3,3,64]{3,0,2,1:T(8,128)}), f32[64,3,3,64]{3,0,2,1:T(8,128)}) %all-reduce.5.cloned.1.call-update) | async-done | bytes 147472 | tf_op jit(solution)/shard_map/psum | solution.py:111
  202.6 1.7 broadcast_multiply_fusion.1
  (63 shorter events, 2.9 us)
Async XLA Ops:
  8.0 42.1 %copy-start = (bf16[128,3,3,256]{3,0,2,1:T(8,128)(2,1)S(1)}, bf16[128,3,3,256]{3,0,2,1:T(8,128)(2,1)}, u32[]{:S(2)}) copy-start(bf16[128,3,3,256]{3,0,2,1:T(8,128)(2,1)} %param.10) | copy-start | bytes 1769476
  8.0 77.5 %reduce-scatter.2.cloned.1.call-start = ((), (), s32[]{:S(2)}) async-start(), calls=%async_computation.1 | async-start | bytes 327680 | tf_op jit(solution)/shard_map/reduce_scatter | solution.py:108
  9.1 6.4 %collective-permute-start = (bf16[64,1,128]{2,0,1:T(8,128)(2,1)S(1)}, bf16[64,1,128]{2,0,1:T(8,128)(2,1)S(1)}, u32[]{:S(2)}, u32[]{:S(2)}) collective-permute-start(bf16[64,1,128]{2,0,1:T(8,128)(2,1)S(1)} %get-tuple-element.58), channel_id=1, source_target_pairs={{0,4},{4,8},{8,12},{1,5},{5,9},{9,13},{2,6},{6,10},{10,14},{3,7},{... | collective-permute-start | bytes 49160 | tf_op jit(solution)/shard_map/ppermute | solution.py:17
  14.0 5.6 %collective-permute-start.1 = (bf16[64,1,128]{2,0,1:T(8,128)(2,1)S(1)}, bf16[64,1,128]{2,0,1:T(8,128)(2,1)S(1)}, u32[]{:S(2)}, u32[]{:S(2)}) collective-permute-start(bf16[64,1,128]{2,0,1:T(8,128)(2,1)S(1)} %get-tuple-element.57), channel_id=1, source_target_pairs={{4,0},{8,4},{12,8},{5,1},{9,5},{13,9},{6,2},{10,6},{14,10},{7,3},{... | collective-permute-start | bytes 49160 | tf_op jit(solution)/shard_map/ppermute | solution.py:19
  19.7 4.4 %collective-permute-start.3 = (bf16[64,10,1]{2,0,1:T(8,128)(2,1)S(1)}, bf16[64,10,1]{2,0,1:T(8,128)(2,1)S(1)}, u32[]{:S(2)}, u32[]{:S(2)}) collective-permute-start(bf16[64,10,1]{2,0,1:T(8,128)(2,1)S(1)} %get-tuple-element.52), channel_id=1, source_target_pairs={{1,0},{2,1},{3,2},{5,4},{6,5},{7,6},{9,8},{10,9},{11,10},{13,12},{... | collective-permute-start | bytes 3848 | tf_op jit(solution)/shard_map/ppermute | solution.py:19
  21.0 4.0 %collective-permute-start.2 = (bf16[64,10,1]{2,0,1:T(8,128)(2,1)S(1)}, bf16[64,10,1]{2,0,1:T(8,128)(2,1)S(1)}, u32[]{:S(2)}, u32[]{:S(2)}) collective-permute-start(bf16[64,10,1]{2,0,1:T(8,128)(2,1)S(1)} %get-tuple-element.51), channel_id=1, source_target_pairs={{0,1},{1,2},{2,3},{4,5},{5,6},{6,7},{8,9},{9,10},{10,11},{12,13},{... | collective-permute-start | bytes 3848 | tf_op jit(solution)/shard_map/ppermute | solution.py:17
  25.6 0.9 copy-start.3
  25.6 0.9 copy-start.4
  28.8 6.4 %collective-permute-start.5 = (bf16[256,1,2]{1,0,2:T(8,128)(2,1)S(1)}, bf16[256,1,2]{1,0,2:T(8,128)(2,1)S(1)}, u32[]{:S(2)}, u32[]{:S(2)}) collective-permute-start(bf16[256,1,2]{1,0,2:T(8,128)(2,1)S(1)} %get-tuple-element.56), channel_id=1, source_target_pairs={{1,0},{2,1},{3,2},{5,4},{6,5},{7,6},{9,8},{10,9},{11,10},{13,12},{... | collective-permute-start | bytes 3080 | tf_op jit(solution)/shard_map/ppermute | solution.py:19
  30.1 5.9 %collective-permute-start.4 = (bf16[256,1,2]{1,0,2:T(8,128)(2,1)S(1)}, bf16[256,1,2]{1,0,2:T(8,128)(2,1)S(1)}, u32[]{:S(2)}, u32[]{:S(2)}) collective-permute-start(bf16[256,1,2]{1,0,2:T(8,128)(2,1)S(1)} %get-tuple-element.55), channel_id=1, source_target_pairs={{0,1},{1,2},{2,3},{4,5},{5,6},{6,7},{8,9},{9,10},{10,11},{12,13},{... | collective-permute-start | bytes 3080 | tf_op jit(solution)/shard_map/ppermute | solution.py:17
  50.1 1.0 copy-start.2
  53.9 4.0 %collective-permute-start.6 = (f32[256,1,8]{0,2,1:T(8,128)S(1)}, f32[256,1,8]{0,2,1:T(8,128)S(1)}, u32[]{:S(2)}, u32[]{:S(2)}) collective-permute-start(f32[256,1,8]{0,2,1:T(8,128)S(1)} %get-tuple-element.48), channel_id=1, source_target_pairs={{0,1},{1,2},{2,3},{4,5},{5,6},{6,7},{8,9},{9,10},{10,11},{12,13},{... | collective-permute-start | bytes 24584 | tf_op jit(solution)/shard_map/ppermute | solution.py:17
  56.6 7.9 %collective-permute-start.7 = (f32[256,1,8]{0,2,1:T(8,128)S(1)}, f32[256,1,8]{0,2,1:T(8,128)S(1)}, u32[]{:S(2)}, u32[]{:S(2)}) collective-permute-start(f32[256,1,8]{0,2,1:T(8,128)S(1)} %get-tuple-element.47), channel_id=1, source_target_pairs={{1,0},{2,1},{3,2},{5,4},{6,5},{7,6},{9,8},{10,9},{11,10},{13,12},{... | collective-permute-start | bytes 24584 | tf_op jit(solution)/shard_map/ppermute | solution.py:19
  65.3 43.0 %all-reduce.7.cloned.1.call-start = ((), (), s32[]{:S(2)}) async-start(), calls=%async_computation.3 | async-start | bytes 2359296 | tf_op jit(solution)/shard_map/psum | solution.py:101
  66.8 135.9 %all-reduce.5.cloned.1.call-start = ((), (), s32[]{:S(2)}) async-start(), calls=%async_computation.2 | async-start | bytes 589824 | tf_op jit(solution)/shard_map/psum | solution.py:111
  86.6 0.9 copy-start.1
  87.7 4.6 %collective-permute-start.8 = (bf16[64,1,128]{2,1,0:T(2,128)(2,1)S(1)}, bf16[64,1,128]{2,1,0:T(2,128)(2,1)S(1)}, u32[]{:S(2)}, u32[]{:S(2)}) collective-permute-start(bf16[64,1,128]{2,1,0:T(2,128)(2,1)S(1)} %get-tuple-element.54), channel_id=1, source_target_pairs={{0,4},{4,8},{8,12},{1,5},{5,9},{9,13},{2,6},{6,10},{10,14},{3,7},{... | collective-permute-start | bytes 49160 | tf_op jit(solution)/shard_map/ppermute | solution.py:17
  89.0 5.8 %collective-permute-start.9 = (bf16[64,1,128]{2,1,0:T(2,128)(2,1)S(1)}, bf16[64,1,128]{2,1,0:T(2,128)(2,1)S(1)}, u32[]{:S(2)}, u32[]{:S(2)}) collective-permute-start(bf16[64,1,128]{2,1,0:T(2,128)(2,1)S(1)} %get-tuple-element.53), channel_id=1, source_target_pairs={{4,0},{8,4},{12,8},{5,1},{9,5},{13,9},{6,2},{10,6},{14,10},{7,3},{... | collective-permute-start | bytes 49160 | tf_op jit(solution)/shard_map/ppermute | solution.py:19
  94.9 5.1 %collective-permute-start.11 = (bf16[64,10,1]{2,0,1:T(8,128)(2,1)S(1)}, bf16[64,10,1]{2,0,1:T(8,128)(2,1)S(1)}, u32[]{:S(2)}, u32[]{:S(2)}) collective-permute-start(bf16[64,10,1]{2,0,1:T(8,128)(2,1)S(1)} %get-tuple-element.50), channel_id=1, source_target_pairs={{1,0},{2,1},{3,2},{5,4},{6,5},{7,6},{9,8},{10,9},{11,10},{13,12},{... | collective-permute-start | bytes 3848 | tf_op jit(solution)/shard_map/ppermute | solution.py:19
  96.2 4.0 %collective-permute-start.10 = (bf16[64,10,1]{2,0,1:T(8,128)(2,1)S(1)}, bf16[64,10,1]{2,0,1:T(8,128)(2,1)S(1)}, u32[]{:S(2)}, u32[]{:S(2)}) collective-permute-start(bf16[64,10,1]{2,0,1:T(8,128)(2,1)S(1)} %get-tuple-element.49), channel_id=1, source_target_pairs={{0,1},{1,2},{2,3},{4,5},{5,6},{6,7},{8,9},{9,10},{10,11},{12,13},{... | collective-permute-start | bytes 3848 | tf_op jit(solution)/shard_map/ppermute | solution.py:17
Sparse Core Ops, SparseCore 0:
  65.4 20.0 reduce-scatter.1
Sparse Core Ops, SparseCore 1:
  68.8 39.4 all-reduce.6
  112.5 90.1 all-reduce.4
where the time goes:
time: 212 us
  waiting for transfers between devices  131 us (62%)
  starting transfers between devices  27.5 us (13%)
  between operations  16.1 us (8%)
  blocking collectives  13.7 us (6%)
  local copies, waits for them, and re-layouts  8.75 us (4%)
  other arithmetic  7.58 us (4%)
  matrix products  7.49 us (4%)
    psum x1, waiting for transfers between devices, local(): lax.psum(local_one, ('row', 'col', 'pair')) / math.sqrt(height * width)  91.9 us
    ppermute x6, starting transfers between devices, padded_2(): lax.ppermute(tail, axis, [(i, (i + 1) % count) for i in range(ends)])  19.6 us
    reduce_scatter x1, waiting for transfers between devices, local(): lax.psum_scatter(real_columns, 'row', scatter_dimension=2, tiled=True)  18.7 us
    all_gather x1, blocking collectives, local(): column_strip = lax.all_gather(with_edges, 'row', axis=2, tiled=True)  13.7 us
    ppermute x6, waiting for transfers between devices, padded_2(): lax.ppermute(head, axis, [((i + 1) % count, i) for i in range(ends)])  12.2 us
    ppermute x6, starting transfers between devices, padded_2(): lax.ppermute(head, axis, [((i + 1) % count, i) for i in range(ends)])  7.75 us
    psum x1, waiting for transfers between devices, local(): lax.psum(local_two, ('col', 'pair'))  5.73 us
    unnamed x21, local copies, waits for them, and re-layouts  5.7 us
  transfers between devices with their start and end apart: 15, of which 10 were waited for; matrix products, arithmetic and copies ran while one was open for 6% of the time, Pallas kernels for 0%

commit v1 on v0

v1 whole, which is shorter than its diff:
```python
import functools
import math

import jax
import jax.numpy as jnp
from jax import lax
from jax.experimental import pallas as pl
from jax.experimental.pallas import tpu as pltpu
from jax.sharding import PartitionSpec as P

MESH = pl.DeviceIdType.MESH
VMEM = pl.BlockSpec(memory_space=pltpu.VMEM)
STRIP = ("col", "pair")


def place():
    return lax.axis_index("row"), lax.axis_index(STRIP)


def device_at(row, strip):
    pairs = lax.axis_size("pair")
    return (lax.axis_index("grp"), row, lax.div(strip, pairs), lax.rem(strip, pairs))


def params(number):
    return pltpu.CompilerParams(
        collective_id=number, has_side_effects=True, vmem_limit_bytes=40 * 1024 * 1024
    )


WAYS = [(a, b) for a in (-1, 0, 1) for b in (-1, 0, 1) if (a, b) != (0, 0)]


def halo_kernel(rows, strips, edge_rows, edge_cols, got_rows, got_cols, got_diag, send_sem, recv_sem):
    row, strip = place()

    def there(way):
        a, b = row + way[0], strip + way[1]
        return (a >= 0) & (a < rows) & (b >= 0) & (b < strips)

    barrier = pltpu.get_barrier_semaphore()
    for way in WAYS:
        @pl.when(there(way))
        def _(way=way):
            pl.semaphore_signal(
                barrier, inc=1, device_id=device_at(row + way[0], strip + way[1]), device_id_type=MESH
            )

    def landing(way):
        if way[1] == 0:
            return got_rows.at[0 if way[0] < 0 else 1]
        if way[0] == 0:
            return got_cols.at[0 if way[1] < 0 else 1]
        return got_diag.at[(0 if way[0] < 0 else 2) + (0 if way[1] < 0 else 1)]

    for way in WAYS:
        @pl.when(jnp.logical_not(there(way)))
        def _(way=way):
            slot = landing(way)
            slot[...] = jnp.zeros(slot.shape, slot.dtype)

    high = 1 + jnp.where(row > 0, 1, 0) + jnp.where(row < rows - 1, 1, 0)
    across = 1 + jnp.where(strip > 0, 1, 0) + jnp.where(strip < strips - 1, 1, 0)
    pl.semaphore_wait(barrier, high * across - 1)

    def copy_to(way):
        back = (-way[0], -way[1])
        if way[1] == 0:
            source = edge_rows.at[0 if way[0] < 0 else 1]
        else:
            source = edge_cols.at[0 if way[1] < 0 else 1]
        return pltpu.make_async_remote_copy(
            src_ref=source,
            dst_ref=landing(back),
            send_sem=send_sem.at[WAYS.index(way)],
            recv_sem=recv_sem.at[WAYS.index(back)],
            device_id=device_at(row + way[0], strip + way[1]),
            device_id_type=MESH,
        )

    for way in WAYS:
        @pl.when(there(way))
        def _(way=way):
            copy_to(way).start()
    for way in WAYS:
        @pl.when(there(way))
        def _(way=way):
            back = (-way[0], -way[1])
            copy_to(way).wait_send()
            copy_to(back).wait_recv()


def halo_exchange(cells, wide, number):
    channels, height, width = cells.shape
    edge_rows = jnp.stack(
        [cells[:, :wide].reshape(channels * wide, width), cells[:, -wide:].reshape(channels * wide, width)]
    )
    flat = jnp.stack(
        [cells[:, :, :wide].reshape(channels, height * wide), cells[:, :, -wide:].reshape(channels, height * wide)]
    )
    edge_cols = jnp.pad(flat, ((0, 0), (0, 0), (0, 128 - height * wide)))
    rows, strips = lax.axis_size("row"), lax.axis_size(STRIP)
    got_rows, got_cols, got_diag = pl.pallas_call(
        functools.partial(halo_kernel, rows, strips),
        out_shape=(
            jax.ShapeDtypeStruct(edge_rows.shape, cells.dtype),
            jax.ShapeDtypeStruct(edge_cols.shape, cells.dtype),
            jax.ShapeDtypeStruct((4,) + edge_cols.shape[1:], cells.dtype),
        ),
        in_specs=[VMEM] * 2,
        out_specs=(VMEM,) * 3,
        scratch_shapes=[pltpu.SemaphoreType.DMA((8,)), pltpu.SemaphoreType.DMA((8,))],
        compiler_params=params(number),
    )(edge_rows, edge_cols)
    got_rows = got_rows.reshape(2, channels, wide, width)
    side = got_cols[:, :, : height * wide].reshape(2, channels, height, wide)
    corner = got_diag[:, :, : height * wide].reshape(4, channels, height, wide)
    above = jnp.concatenate([corner[0, :, -wide:], got_rows[0], corner[1, :, -wide:]], 2)
    middle = jnp.concatenate([side[0], cells, side[1]], 2)
    below = jnp.concatenate([corner[2, :, :wide], got_rows[1], corner[3, :, :wide]], 2)
    return jnp.concatenate([above, middle, below], 1)


def greet(count, me, device_of):
    barrier = pltpu.get_barrier_semaphore()

    @pl.loop(1, count)
    def _(step):
        pl.semaphore_signal(
            barrier, inc=1, device_id=device_of(lax.rem(me + step, count)), device_id_type=MESH
        )

    pl.semaphore_wait(barrier, count - 1)


def post(count, me, device_of, source, landing, send_sem, recv_sem):
    def copy_of(step):
        peer = lax.rem(me + step, count)
        return pltpu.make_async_remote_copy(
            src_ref=source(peer),
            dst_ref=landing.at[me],
            send_sem=send_sem.at[step],
            recv_sem=recv_sem.at[me],
            device_id=device_of(peer),
            device_id_type=MESH,
        )

    def arrival(step):
        peer = lax.rem(me + step, count)
        return pltpu.make_async_remote_copy(
            src_ref=source(peer),
            dst_ref=landing.at[peer],
            send_sem=send_sem.at[step],
            recv_sem=recv_sem.at[peer],
            device_id=device_of(peer),
            device_id_type=MESH,
        )

    @pl.loop(1, count)
    def _(step):
        copy_of(step).start()

    def finish():
        @pl.loop(1, count)
        def _(step):
            copy_of(step).wait_send()
            arrival(step).wait_recv()

    return finish


def group(kind):
    rows, strips = lax.axis_size("row"), lax.axis_size(STRIP)
    row, strip = place()
    if kind == "all":
        return (
            rows * strips,
            row * strips + strip,
            lambda i: device_at(lax.div(i, strips), lax.rem(i, strips)),
        )
    if kind == "strips":
        return strips, strip, lambda i: device_at(row, i)
    return rows, row, lambda i: device_at(i, strip)


def gather_kernel(kind, block, out, send_sem, recv_sem):
    count, me, device_of = group(kind)
    greet(count, me, device_of)
    finish = post(count, me, device_of, lambda peer: block, out, send_sem, recv_sem)
    out[me] = block[...]
    finish()


def sems(count):
    return [pltpu.SemaphoreType.DMA((count,)), pltpu.SemaphoreType.DMA((count,))]


def group_size(kind):
    rows, strips = lax.axis_size("row"), lax.axis_size(STRIP)
    return dict(all=rows * strips, strips=strips, rows=rows)[kind]


def gather(block, kind, number):
    count = group_size(kind)
    return pl.pallas_call(
        functools.partial(gather_kernel, kind),
        out_shape=jax.ShapeDtypeStruct((count,) + block.shape, block.dtype),
        in_specs=[VMEM],
        out_specs=VMEM,
        scratch_shapes=sems(count),
        compiler_params=params(number),
    )(block)


def total_of(count, landing):
    return lax.fori_loop(
        1,
        count,
        lambda i, value: value + landing[i].astype(jnp.float32),
        landing[0].astype(jnp.float32),
    )


def scatter_kernel(kind, blocks, out, landing, send_sem, recv_sem):
    count, me, device_of = group(kind)
    greet(count, me, device_of)
    finish = post(count, me, device_of, lambda peer: blocks.at[peer], landing, send_sem, recv_sem)
    landing[me] = blocks[me]
    finish()
    out[...] = total_of(count, landing)


def reduce_scatter(blocks, kind, number):
    count = group_size(kind)
    return pl.pallas_call(
        functools.partial(scatter_kernel, kind),
        out_shape=jax.ShapeDtypeStruct(blocks.shape[1:], jnp.float32),
        in_specs=[VMEM],
        out_specs=VMEM,
        scratch_shapes=[pltpu.VMEM(blocks.shape, blocks.dtype)] + sems(count),
        compiler_params=params(number),
    )(blocks)


def all_reduce_kernel(kind, blocks, out, landing, mine, send_sem, recv_sem, send_two, recv_two):
    count, me, device_of = group(kind)
    greet(count, me, device_of)
    finish = post(count, me, device_of, lambda peer: blocks.at[peer], landing, send_sem, recv_sem)
    landing[me] = blocks[me]
    finish()
    total = total_of(count, landing).astype(mine.dtype)
    mine[...] = total
    finish = post(count, me, device_of, lambda peer: mine, out, send_two, recv_two)
    out[me] = total
    finish()


def all_reduce(blocks, kind, number):
    count = group_size(kind)
    return pl.pallas_call(
        functools.partial(all_reduce_kernel, kind),
        out_shape=jax.ShapeDtypeStruct(blocks.shape, blocks.dtype),
        in_specs=[VMEM],
        out_specs=VMEM,
        scratch_shapes=[pltpu.VMEM(blocks.shape, blocks.dtype), pltpu.VMEM(blocks.shape[1:], blocks.dtype)]
        + sems(count)
        + sems(count),
        compiler_params=params(number),
    )(blocks)


def conv_valid(cells, kernel, numbers):
    return lax.conv_general_dilated(
        cells[None], kernel, (1, 1), "VALID", dimension_numbers=numbers, preferred_element_type=jnp.float32
    )[0]


def flip_kernel(kernel):
    return jnp.transpose(kernel[:, ::-1, ::-1, :], (3, 1, 2, 0))


def silu_slope(values):
    sigmoid_value = jax.nn.sigmoid(values)
    return sigmoid_value * (1.0 + values * (1.0 - sigmoid_value))


def tap_grads(gradient, padded, letters):
    row_count, col_count = gradient.shape[:2]
    taps = []
    for first in range(3):
        for second in range(3):
            if letters == "chw":
                window = padded[:, first : first + row_count, second : second + col_count]
            else:
                window = padded[first : first + row_count, second : second + col_count]
            taps.append(
                jnp.einsum("hwo," + letters + "->oc", gradient, window, preferred_element_type=jnp.float32)
            )
    return jnp.stack(taps, 1)


def local(features_in, filters_one, filters_two, out_grad):
    channels, band, width = features_in.shape
    rows, strips = lax.axis_size("row"), lax.axis_size(STRIP)
    row, strip = place()
    quads = channels * 4
    band2, width2 = band // 4, width // 4
    height2, full2 = band2 * rows, width2 * strips
    filters = filters_two.shape[0]

    features = halo_exchange(features_in, 2, 0)
    pre_one = conv_valid(features, filters_one, ("NCHW", "OHWI", "NHWC"))
    active = jax.nn.silu(pre_one[1:-1, 1:-1])
    pooled = active.reshape(band2, 2, 2, width2, 2, 2, channels).mean(axis=(2, 5))
    pooled = jnp.transpose(pooled, (0, 2, 4, 1, 3)).astype(jnp.bfloat16)
    pooled = pooled.reshape(band2 * width2, quads)

    gathered = gather(pooled, "all", 1).reshape(rows, strips, band2, width2, quads)
    whole = jnp.transpose(gathered, (0, 2, 1, 3, 4)).reshape(height2, full2, quads)
    whole = jnp.pad(whole, ((1, 1), (1, 1), (0, 0)))
    own = lax.dynamic_slice_in_dim(whole, strip * width2, width2 + 2, 1)
    pre_two = conv_valid(own, filters_two, ("NHWC", "OHWI", "NHWC"))
    upstream = jnp.transpose(out_grad, (2, 1, 0)).astype(jnp.float32)
    grad_two_own = (upstream * silu_slope(pre_two)).astype(jnp.bfloat16)

    strips_got = gather(grad_two_own.reshape(height2 * width2, filters), "strips", 2)
    grad_pre_two = jnp.transpose(
        strips_got.reshape(strips, height2, width2, filters), (1, 0, 2, 3)
    ).reshape(height2, full2, filters)

    near = lax.dynamic_slice_in_dim(
        jnp.pad(grad_pre_two, ((1, 1), (2, 2), (0, 0))), strip * width2, width2 + 4, 1
    )
    spread = conv_valid(near, flip_kernel(filters_two), ("NHWC", "OHWI", "NHWC"))
    channel = jnp.arange(quads)
    low_row = (channel // 2) % 2 == 1
    low_col = channel % 2 == 1
    tall = jnp.pad(spread, ((1, 1), (0, 0), (0, 0)))
    bands = spread.reshape(rows, band2, width2 + 2, quads)
    rim = jnp.where(
        low_row, tall[0 : height2 : band2], tall[band2 + 1 : height2 + 2 : band2]
    )
    bands = jnp.concatenate([bands, rim[:, None]], 1)
    edge = jnp.where(low_col, bands[:, :, :1], bands[:, :, -1:])
    bands = jnp.concatenate([bands[:, :, 1:-1], edge], 2).astype(jnp.bfloat16)
    spots = (band2 + 1) * (width2 + 1)
    room = -(-spots // 16) * 16
    bands = jnp.pad(bands.reshape(rows, spots, quads), ((0, 0), (0, room - spots), (0, 0)))
    grad_pooled = reduce_scatter(bands, "rows", 3)[:spots]

    grad_two = tap_grads(grad_pre_two, whole, "hwc") * (1.0 / math.sqrt(height2 * full2))
    grad_two = grad_two.reshape(filters, 3, 3, quads)

    halves = jnp.transpose(
        grad_pooled.reshape(band2 + 1, width2 + 1, channels, 2, 2), (0, 3, 1, 4, 2)
    ).reshape(2 * band2 + 2, 2 * width2 + 2, channels)
    halves = jnp.roll(halves, (1, 1), (0, 1))
    wide = jnp.repeat(jnp.repeat(halves, 2, 0), 2, 1)[1:-1, 1:-1] * 0.25
    at_row = row * band - 1 + jnp.arange(band + 2)
    at_col = strip * width - 1 + jnp.arange(width + 2)
    inside = ((at_row >= 0) & (at_row < band * rows))[:, None] & (
        (at_col >= 0) & (at_col < width * strips)
    )[None]
    grad_ext = jnp.where(inside[:, :, None], wide * silu_slope(pre_one), 0.0).astype(jnp.bfloat16)

    local_one = tap_grads(grad_ext[1:-1, 1:-1], features[:, 1:-1, 1:-1], "chw")
    local_one = local_one * (1.0 / math.sqrt(band * rows * width * strips))
    count = rows * strips
    cells = channels * 9 * channels
    piece = -(-cells // (count * 128 * 16)) * 16
    flat = jnp.pad(local_one.reshape(-1).astype(jnp.bfloat16), (0, count * piece * 128 - cells))
    summed = all_reduce(flat.reshape(count, piece, 128), "all", 4)
    grad_one = summed.reshape(-1)[:cells].reshape(channels, 3, 3, channels).astype(jnp.float32)

    input_grad = conv_valid(grad_ext, flip_kernel(filters_one), ("NHWC", "OHWI", "NCHW")).astype(jnp.bfloat16)
    return (input_grad, grad_one, grad_two)


def solution(mesh):
    in_specs = (
        P("grp", "row", ("col", "pair")),
        P(),
        P("row", None, None, None),
        P(("grp", "row"), ("col", "pair"), None),
    )
    out_specs = (
        P("grp", "row", ("col", "pair")),
        P("grp", None, None, None),
        P(("grp", "row"), None, None, None),
    )
    return jax.shard_map(local, mesh=mesh, in_specs=in_specs, out_specs=out_specs, check_vma=False)
```

time: 212 us -> 86.3 us (0.41)
  waiting for transfers between devices: 131 us -> 0 us
  Pallas kernels: 0 us -> 52.1 us
  starting transfers between devices: 27.5 us -> 0 us
  between operations: 16.1 us -> 1.56 us
  blocking collectives: 13.7 us -> 0 us
  local copies, waits for them, and re-layouts: 8.75 us -> 15.4 us
  matrix products: 7.49 us -> 13.4 us
  other arithmetic: 7.58 us -> 3.56 us
    psum x2 -> x0, waiting for transfers between devices: 97.6 us -> none  [the longest x1 91.9 us: local(): lax.psum(local_one, ('row', 'col', 'pair')) / math.sqrt(height * width)]
    pallas_call x0 -> x5, Pallas kernels: none -> 52.1 us  [the longest x2 19.5 us: gather(): pl.pallas_call(functools.partial(gather_kernel, kind), out_shape=jax.Shap...]
    ppermute x12 -> x0, starting transfers between devices: 27.4 us -> none  [the longest x6 19.6 us: padded_2(): lax.ppermute(tail, axis, [(i, (i + 1) % count) for i in range(ends)])]
    reduce_scatter x1 -> x0, waiting for transfers between devices: 18.7 us -> none  [local(): lax.psum_scatter(real_columns, 'row', scatter_dimension=2, tiled=True)]
    ppermute x12 -> x0, waiting for transfers between devices: 14.3 us -> none  [the longest x6 12.2 us: padded_2(): lax.ppermute(head, axis, [((i + 1) % count, i) for i in range(ends)])]
    all_gather x1 -> x0, blocking collectives: 13.7 us -> none  [local(): column_strip = lax.all_gather(with_edges, 'row', axis=2, tiled=True)]
    conv_general_dilated x4, matrix products: 3.4 us -> 8.42 us  [conv_valid(): lax.conv_general_dilated(cells[None], kernel, (1, 1), 'VALID', dimension_...]
    slice x7 -> x17, local copies, waits for them, and re-layouts: 0.41 us -> 4.86 us  [the longest x2 1.23 us: halo_exchange(): cells[:, :, :wide].reshape(channels, height * wide)]
  transfers between devices with their start and end apart: 15 -> 0, of which waited for: 10 -> 0; matrix products, arithmetic and copies ran while one was open for 6% -> 0% of each run, Pallas kernels for 0% -> 0%
where the time goes in v1:
time: 86.3 us; the launch traced here: 86 us
  Pallas kernels  52.1 us (60%)
  local copies, waits for them, and re-layouts  15.4 us (18%)
  matrix products  13.4 us (16%)
  other arithmetic  3.56 us (4%)
  between operations  1.56 us (2%)
    pallas_call x2, Pallas kernels, gather(): pl.pallas_call(functools.partial(gather_kernel, kind), out_shape=jax.Shap...  19.5 us
    pallas_call x1, Pallas kernels, all_reduce(): pl.pallas_call(functools.partial(all_reduce_kernel, kind), out_shape=jax....  14.7 us
    pallas_call x1, Pallas kernels, reduce_scatter(): pl.pallas_call(functools.partial(scatter_kernel, kind), out_shape=jax.Sha...  10.9 us
    conv_general_dilated x4, matrix products, conv_valid(): lax.conv_general_dilated(cells[None], kernel, (1, 1), 'VALID', dimension_...  8.42 us
    pallas_call x1, Pallas kernels, halo_exchange(): pl.pallas_call(functools.partial(halo_kernel, rows, strips), out_shape=(j...  6.94 us
    dot_general x18, matrix products, tap_grads(): jnp.einsum('hwo,' + letters + '->oc', gradient, window, preferred_element...  4.94 us
    unnamed x52, local copies, waits for them, and re-layouts  3.49 us

profile of v1, /device:TPU:0, one launch (start us, length us, event | category | flops | bytes accessed | tf_op | source)
XLA Modules:
  0.0 86.0 jit_solution(11105280396008772395)
XLA Ops:
  0.7 1.1 %fusion.78 = (bf16[64,2,128]{2,1,0:T(2,128)(2,1)S(1)}, bf16[64,2,128]{2,1,0:T(2,128)(2,1)S(1)}) fusion(bf16[64,8,128]{2,1,0:T(8,128)(2,1)} %param.4), kind=kLoop, calls=%fused_computation.143 | loop fusion | bytes 131072 | tf_op jit(solution)/shard_map/slice | solution.py:96
  1.8 1.1 %fusion.77 = (bf16[64,8,2]{2,1,0:T(8,128)(2,1)S(1)}, bf16[64,8,2]{2,1,0:T(8,128)(2,1)S(1)}) fusion(bf16[64,8,128]{2,1,0:T(8,128)(2,1)} %param.4), kind=kLoop, calls=%fused_computation.142 | loop fusion | bytes 8192 | tf_op jit(solution)/shard_map/slice | solution.py:99
  2.9 0.2 copy.151
  3.0 0.2 copy.150
  3.3 6.9 %shard_map.67 = (bf16[2,128,128]{2,1,0:T(8,128)(2,1)S(1)}, bf16[2,64,128]{2,1,0:T(8,128)(2,1)S(1)}, bf16[4,64,128]{2,1,0:T(8,128)(2,1)S(1)}) custom-call(bf16[2,128,128]{2,1,0:T(8,128)(2,1)S(1)} %pad_maximum_fusion.7.edge_rows, bf16[2,64,128]{2,1,0:T(8,128)(2,1)S(1)} %pad.24.edge_cols), custom_call_target="tpu_custom_call" | custom-call | tf_op jit(solution)/shard_map/pallas_call | solution.py:103
  10.4 0.1 copy.216
  10.5 0.1 copy.215
  10.8 0.2 copy.161
  11.1 0.2 copy.159
  11.2 0.1 copy.214
  11.4 0.1 copy.213
  11.5 0.3 maximum_bitcast_fusion
  11.8 0.9 %copy.165 = bf16[1,64,12,132]{1,0,3,2:T(2,128)(2,1)S(1)} copy(bf16[1,64,12,132]{3,1,2,0:T(8,128)(2,1)S(1)} %maximum_bitcast_fusion) | data formatting | bytes 405504 | tf_op jit(solution)/shard_map/broadcast_in_dim | solution.py:274
  12.7 5.8 %fusion.82 = f32[1,10,130,64]{3,0,2,1:T(1,128)} fusion(bf16[1,64,12,132]{1,0,3,2:T(2,128)(2,1)S(1)} %copy.165, bf16[64,3,3,64]{3,0,2,1:T(8,128)(2,1)S(1)} %copy-done.18), kind=kOutput, calls=%fused_computation.147 | convolution fusion | flops 95846400 | bytes 609280 | tf_op jit(solution)/shard_map/conv_general_dilated | solution.py:273
  18.5 1.5 %copy.166 = f32[1,10,130,64]{2,3,1,0:T(8,128)S(1)} copy(f32[1,10,130,64]{3,0,2,1:T(1,128)} %fusion.82) | data formatting | bytes 665600 | tf_op jit(solution)/shard_map/conv_general_dilated | solution.py:273
  20.0 0.1 divide_multiply_fusion
  20.2 0.2 copy.167
  20.4 0.5 reduce_sum.9
  21.0 0.1 copy.168
  21.3 13.4 %shard_map.68 = bf16[16,64,256]{2,1,0:T(8,128)(2,1)S(1)} custom-call(bf16[64,256]{1,0:T(8,128)(2,1)S(1)} %copy.169.block), custom_call_target="tpu_custom_call" | custom-call | tf_op jit(solution)/shard_map/pallas_call | solution.py:205
  34.9 1.0 %fusion.28 = f32[1,8,32,128]{3,0,2,1:T(1,128)S(1)} fusion(bf16[128,3,3,256]{3,0,2,1:T(8,128)(2,1)S(1)} %copy-done, bf16[1,10,34,256]{3,2,1,0:T(8,128)(2,1)S(1)} %fusion.31), kind=kOutput, calls=%fused_computation.64 | convolution fusion | flops 150994944 | bytes 894976 | tf_op jit(solution)/shard_map/conv_general_dilated | solution.py:273
  36.0 6.1 %shard_map.69 = bf16[4,256,128]{2,1,0:T(8,128)(2,1)S(1)} custom-call(bf16[256,128]{1,0:T(8,128)(2,1)S(1)} %bitcast.175), custom_call_target="tpu_custom_call" | custom-call | tf_op jit(solution)/shard_map/pallas_call | solution.py:205
  42.2 1.0 %fusion.33 = bf16[1,8,34,256]{3,0,2,1:T(2,128)(2,1)S(1)} fusion(bf16[128,3,3,256]{3,0,2,1:T(8,128)(2,1)S(1)} %copy-done, bf16[1,10,36,128]{3,2,1,0:T(8,128)(2,1)S(1)} %fusion.44), kind=kOutput, calls=%fused_computation.78 | convolution fusion | flops 160432128 | bytes 821248 | tf_op jit(solution)/shard_map/conv_general_dilated | solution.py:273
  43.3 0.4 slice.179
  43.7 0.4 slice.180
  44.5 0.3 fusion.21
  44.8 0.2 pad_maximum_fusion
  45.1 10.9 %shard_map.70 = f32[112,256]{1,0:T(8,128)S(1)} custom-call(bf16[4,112,256]{2,1,0:T(8,128)(2,1)S(1)} %pad.28.blocks), custom_call_target="tpu_custom_call" | custom-call | tf_op jit(solution)/shard_map/pallas_call | solution.py:235
  56.2 0.2 reshape.123
  56.4 0.3 copy.179
  56.7 0.1 reshape.124
  56.9 0.3 broadcast_in_dim.52
  57.2 1.5 %reshape.126 = f32[12,132,64]{2,1,0:T(8,128)} reshape(f32[12,66,2,64]{3,2,1,0:T(2,128)S(1)} %broadcast_in_dim.52) | data formatting | bytes 811008 | tf_op jit(solution)/shard_map/reshape | solution.py:358
  58.7 1.1 %slice.221 = f32[10,130,64]{2,1,0:T(8,128)S(1)} slice(f32[12,132,64]{2,1,0:T(8,128)} %reshape.126), slice={[1:11], [1:131], [0:64]} | slice | bytes 665600 | tf_op jit(solution)/shard_map/slice | solution.py:358
  59.8 0.4 copy.217
  60.3 0.3 select_convert_fusion
  60.6 0.3 copy.218
  61.2 0.6 copy-done.19
  61.8 0.6 fusion
  62.5 0.9 %copy.200 = bf16[64,8,128]{2,1,0:T(8,128)(2,1)} copy(bf16[64,8,128]{0,1,2:T(8,128)(2,1)S(1)} %slice_bitcast_fusion) | data formatting | bytes 262144
  63.5 0.3 maximum_maximum_fusion.1
  63.8 0.3 fusion.18
  64.1 0.3 fusion.17
  64.3 0.3 fusion.16
  64.6 0.3 fusion.15
  64.9 0.2 fusion.14
  65.1 0.3 fusion.13
  65.4 0.3 fusion.12
  65.7 0.3 fusion.11
  66.0 0.3 fusion.10
  66.4 0.2 convert_element_type.63
  66.6 14.7 %shard_map.71 = bf16[16,32,128]{2,1,0:T(8,128)(2,1)S(1)} custom-call(bf16[16,32,128]{2,1,0:T(8,128)(2,1)S(1)} %bitcast.174), custom_call_target="tpu_custom_call" | custom-call | tf_op jit(solution)/shard_map/pallas_call | solution.py:260
  81.3 0.2 reshape.135
  81.5 0.7 copy.201
  82.2 0.3 fusion.9
  82.5 0.3 fusion.8
  82.8 0.3 fusion.7
  83.1 0.3 fusion.6
  83.4 0.3 fusion.5
  83.7 0.3 fusion.4
  84.0 0.3 fusion.3
  84.3 0.3 fusion.2
  84.6 0.3 fusion.1
  84.9 1.1 %broadcast_multiply_fusion = f32[128,9,256]{2,0,1:T(8,128)} fusion(f32[128,9,256]{2,0,1:T(8,128)S(1)} %fusion.1), kind=kLoop, calls=%fused_computation.54 | loop fusion | flops 294912 | bytes 2359296 | tf_op jit(solution)/shard_map/mul | solution.py:351
  (93 shorter events, 2.3 us)
Async XLA Ops:
  0.6 34.2 %copy-start = (bf16[128,3,3,256]{3,0,2,1:T(8,128)(2,1)S(1)}, bf16[128,3,3,256]{3,0,2,1:T(8,128)(2,1)}, u32[]{:S(2)}) copy-start(bf16[128,3,3,256]{3,0,2,1:T(8,128)(2,1)} %param.6) | copy-start | bytes 1769476
  0.6 10.3 %copy-start.5 = (bf16[64,8,128]{2,1,0:T(8,128)(2,1)S(1)}, bf16[64,8,128]{2,1,0:T(8,128)(2,1)}, u32[]{:S(2)}) copy-start(bf16[64,8,128]{2,1,0:T(8,128)(2,1)} %param.4) | copy-start | bytes 393220
  10.5 2.1 %copy-start.7 = (bf16[64,2,128]{2,0,1:T(8,128)(2,1)}, bf16[64,2,128]{2,0,1:T(8,128)(2,1)S(1)}, u32[]{:S(2)}) copy-start(bf16[64,2,128]{2,0,1:T(8,128)(2,1)S(1)} %copy.164) | copy-start | bytes 98308
  10.7 2.0 %copy-start.9 = (bf16[1,64,2,2]{3,1,2,0:T(8,128)(2,1)}, bf16[1,64,2,2]{3,1,2,0:T(8,128)(2,1)S(1)}, u32[]{:S(2)}) copy-start(bf16[1,64,2,2]{3,1,2,0:T(8,128)(2,1)S(1)} %copy.215) | copy-start | bytes 1540
  10.9 1.8 %copy-start.1 = (bf16[64,8,2]{2,0,1:T(8,128)(2,1)}, bf16[64,8,2]{2,0,1:T(8,128)(2,1)S(1)}, u32[]{:S(2)}) copy-start(bf16[64,8,2]{2,0,1:T(8,128)(2,1)S(1)} %copy.161) | copy-start | bytes 6148
  11.2 7.3 %copy-start.3 = (bf16[64,8,2]{2,0,1:T(8,128)(2,1)}, bf16[64,8,2]{2,0,1:T(8,128)(2,1)S(1)}, u32[]{:S(2)}) copy-start(bf16[64,8,2]{2,0,1:T(8,128)(2,1)S(1)} %copy.159) | copy-start | bytes 6148
  11.2 1.5 %copy-start.18 = (bf16[64,3,3,64]{3,0,2,1:T(8,128)(2,1)S(1)}, bf16[64,3,3,64]{3,0,2,1:T(8,128)(2,1)}, u32[]{:S(2)}) copy-start(bf16[64,3,3,64]{3,0,2,1:T(8,128)(2,1)} %param.5) | copy-start | bytes 221188
  11.4 7.2 %copy-start.11 = (bf16[1,64,2,2]{3,1,2,0:T(8,128)(2,1)}, bf16[1,64,2,2]{3,1,2,0:T(8,128)(2,1)S(1)}, u32[]{:S(2)}) copy-start(bf16[1,64,2,2]{3,1,2,0:T(8,128)(2,1)S(1)} %copy.214) | copy-start | bytes 1540
  11.4 7.2 %copy-start.13 = (bf16[64,2,128]{2,0,1:T(8,128)(2,1)}, bf16[64,2,128]{2,0,1:T(8,128)(2,1)S(1)}, u32[]{:S(2)}) copy-start(bf16[64,2,128]{2,0,1:T(8,128)(2,1)S(1)} %copy.156) | copy-start | bytes 98308
  11.5 1.2 %copy-start.15 = (bf16[1,64,2,2]{3,1,2,0:T(8,128)(2,1)}, bf16[1,64,2,2]{3,1,2,0:T(8,128)(2,1)S(1)}, u32[]{:S(2)}) copy-start(bf16[1,64,2,2]{3,1,2,0:T(8,128)(2,1)S(1)} %copy.213) | copy-start | bytes 1540
  34.9 1.1 %copy-start.17 = (bf16[128,32,8]{0,2,1:T(8,128)(2,1)S(1)}, bf16[128,32,8]{0,2,1:T(8,128)(2,1)}, u32[]{:S(2)}) copy-start(bf16[128,32,8]{0,2,1:T(8,128)(2,1)} %param.7) | copy-start | bytes 196612
  60.9 0.9 %copy-start.19 = (bf16[64,3,3,64]{3,0,2,1:T(8,128)(2,1)S(1)}, bf16[64,3,3,64]{3,0,2,1:T(8,128)(2,1)}, u32[]{:S(2)}) copy-start(bf16[64,3,3,64]{3,0,2,1:T(8,128)(2,1)} %param.5) | copy-start | bytes 221188
  60.9 0.9 %copy-start.20 = (pred[8,17]{0,1:T(8,128)(4,1)S(1)}, pred[8,17]{0,1:T(8,128)(4,1)}, u32[]{:S(2)}) copy-start(pred[8,17]{0,1:T(8,128)(4,1)} %constant.99) | copy-start | bytes 412
  62.4 1.0 %copy-start.2 = (bf16[64,8,2]{2,0,1:T(8,128)(2,1)S(1)}, bf16[64,8,2]{2,0,1:T(8,128)(2,1)}, u32[]{:S(2)}) copy-start(bf16[64,8,2]{2,0,1:T(8,128)(2,1)} %copy-done.1) | copy-start | bytes 6148
  62.4 1.0 %copy-start.4 = (bf16[64,8,2]{2,0,1:T(8,128)(2,1)S(1)}, bf16[64,8,2]{2,0,1:T(8,128)(2,1)}, u32[]{:S(2)}) copy-start(bf16[64,8,2]{2,0,1:T(8,128)(2,1)} %copy-done.3) | copy-start | bytes 6148
  62.4 1.0 %copy-start.8 = (bf16[64,2,128]{2,0,1:T(8,128)(2,1)S(1)}, bf16[64,2,128]{2,0,1:T(8,128)(2,1)}, u32[]{:S(2)}) copy-start(bf16[64,2,128]{2,0,1:T(8,128)(2,1)} %copy-done.7) | copy-start | bytes 98308
  62.4 1.0 %copy-start.10 = (bf16[1,64,2,2]{3,1,2,0:T(8,128)(2,1)S(1)}, bf16[1,64,2,2]{3,1,2,0:T(8,128)(2,1)}, u32[]{:S(2)}) copy-start(bf16[1,64,2,2]{3,1,2,0:T(8,128)(2,1)} %copy-done.9) | copy-start | bytes 1540
  62.4 1.0 %copy-start.12 = (bf16[1,64,2,2]{3,1,2,0:T(8,128)(2,1)S(1)}, bf16[1,64,2,2]{3,1,2,0:T(8,128)(2,1)}, u32[]{:S(2)}) copy-start(bf16[1,64,2,2]{3,1,2,0:T(8,128)(2,1)} %copy-done.11) | copy-start | bytes 1540
  62.4 1.0 %copy-start.14 = (bf16[64,2,128]{2,0,1:T(8,128)(2,1)S(1)}, bf16[64,2,128]{2,0,1:T(8,128)(2,1)}, u32[]{:S(2)}) copy-start(bf16[64,2,128]{2,0,1:T(8,128)(2,1)} %copy-done.13) | copy-start | bytes 98308
  62.5 1.0 %copy-start.16 = (bf16[1,64,2,2]{3,1,2,0:T(8,128)(2,1)S(1)}, bf16[1,64,2,2]{3,1,2,0:T(8,128)(2,1)}, u32[]{:S(2)}) copy-start(bf16[1,64,2,2]{3,1,2,0:T(8,128)(2,1)} %copy-done.15) | copy-start | bytes 1540
  63.4 1.5 %copy-start.6 = (bf16[64,8,128]{2,1,0:T(8,128)(2,1)S(1)}, bf16[64,8,128]{2,1,0:T(8,128)(2,1)}, u32[]{:S(2)}) copy-start(bf16[64,8,128]{2,1,0:T(8,128)(2,1)} %param.4) | copy-start | bytes 393220

commit v2 on v1

v2 whole, which is shorter than its diff:
```python
import functools
import math

import jax
import jax.numpy as jnp
from jax import lax
from jax.experimental import pallas as pl
from jax.experimental.pallas import tpu as pltpu
from jax.sharding import PartitionSpec as P

MESH = pl.DeviceIdType.MESH
VMEM = pl.BlockSpec(memory_space=pltpu.VMEM)
STRIP = ("col", "pair")


def place():
    return lax.axis_index("row"), lax.axis_index(STRIP)


def device_at(row, strip):
    pairs = lax.axis_size("pair")
    return (lax.axis_index("grp"), row, lax.div(strip, pairs), lax.rem(strip, pairs))


def params(number):
    return pltpu.CompilerParams(
        collective_id=number, has_side_effects=True, vmem_limit_bytes=40 * 1024 * 1024
    )


WAYS = [(a, b) for a in (-1, 0, 1) for b in (-1, 0, 1) if (a, b) != (0, 0)]


def halo_kernel(
    rows, strips, edge_rows, edge_cols, edge_up, got_rows, got_cols, got_diag, got_up, send_sem, recv_sem
):
    row, strip = place()

    def there(way):
        a, b = row + way[0], strip + way[1]
        return (a >= 0) & (a < rows) & (b >= 0) & (b < strips)

    barrier = pltpu.get_barrier_semaphore()
    for way in WAYS:
        @pl.when(there(way))
        def _(way=way):
            pl.semaphore_signal(
                barrier, inc=1, device_id=device_at(row + way[0], strip + way[1]), device_id_type=MESH
            )

    def landing(way):
        if way[1] == 0:
            return got_rows.at[0 if way[0] < 0 else 1]
        if way[0] == 0:
            return got_cols.at[0 if way[1] < 0 else 1]
        return got_diag.at[(0 if way[0] < 0 else 2) + (0 if way[1] < 0 else 1)]

    for way in WAYS:
        @pl.when(jnp.logical_not(there(way)))
        def _(way=way):
            slot = landing(way)
            slot[...] = jnp.zeros(slot.shape, slot.dtype)
            if way[0] == 0:
                slot = got_up.at[0 if way[1] < 0 else 1]
                slot[...] = jnp.zeros(slot.shape, slot.dtype)

    high = 1 + jnp.where(row > 0, 1, 0) + jnp.where(row < rows - 1, 1, 0)
    across = 1 + jnp.where(strip > 0, 1, 0) + jnp.where(strip < strips - 1, 1, 0)
    pl.semaphore_wait(barrier, high * across - 1)

    def copy_to(way):
        back = (-way[0], -way[1])
        if way[1] == 0:
            source = edge_rows.at[0 if way[0] < 0 else 1]
        else:
            source = edge_cols.at[0 if way[1] < 0 else 1]
        return pltpu.make_async_remote_copy(
            src_ref=source,
            dst_ref=landing(back),
            send_sem=send_sem.at[WAYS.index(way)],
            recv_sem=recv_sem.at[WAYS.index(back)],
            device_id=device_at(row + way[0], strip + way[1]),
            device_id_type=MESH,
        )

    def upstream_to(way):
        side = 0 if way[1] < 0 else 1
        return pltpu.make_async_remote_copy(
            src_ref=edge_up.at[side],
            dst_ref=got_up.at[1 - side],
            send_sem=send_sem.at[8 + side],
            recv_sem=recv_sem.at[9 - side],
            device_id=device_at(row, strip + way[1]),
            device_id_type=MESH,
        )

    for way in WAYS:
        @pl.when(there(way))
        def _(way=way):
            copy_to(way).start()
            if way[0] == 0:
                upstream_to(way).start()
    for way in WAYS:
        @pl.when(there(way))
        def _(way=way):
            back = (-way[0], -way[1])
            copy_to(way).wait_send()
            copy_to(back).wait_recv()
            if way[0] == 0:
                upstream_to(way).wait_send()
                upstream_to(back).wait_recv()


def pad_lanes(cells):
    return jnp.pad(cells, [(0, 0)] * (cells.ndim - 1) + [(0, -cells.shape[-1] % 128)])


def halo_exchange(cells, upstream, tall, wide, number):
    channels, height, width = cells.shape
    filters, count, height2 = upstream.shape
    edge_rows = jnp.stack(
        [cells[:, :tall].reshape(channels * tall, width), cells[:, -tall:].reshape(channels * tall, width)]
    )
    edge_cols = pad_lanes(
        jnp.stack(
            [cells[:, :, :wide].reshape(channels, height * wide), cells[:, :, -wide:].reshape(channels, height * wide)]
        )
    )
    edge_up = pad_lanes(
        jnp.stack(
            [upstream[:, :2].reshape(filters, 2 * height2), upstream[:, -2:].reshape(filters, 2 * height2)]
        )
    )
    rows, strips = lax.axis_size("row"), lax.axis_size(STRIP)
    got_rows, got_cols, got_diag, got_up = pl.pallas_call(
        functools.partial(halo_kernel, rows, strips),
        out_shape=(
            jax.ShapeDtypeStruct(edge_rows.shape, cells.dtype),
            jax.ShapeDtypeStruct(edge_cols.shape, cells.dtype),
            jax.ShapeDtypeStruct((4,) + edge_cols.shape[1:], cells.dtype),
            jax.ShapeDtypeStruct(edge_up.shape, cells.dtype),
        ),
        in_specs=[VMEM] * 3,
        out_specs=(VMEM,) * 4,
        scratch_shapes=[pltpu.SemaphoreType.DMA((10,)), pltpu.SemaphoreType.DMA((10,))],
        compiler_params=params(number),
    )(edge_rows, edge_cols, edge_up)
    got_rows = got_rows.reshape(2, channels, tall, width)
    side = got_cols[:, :, : height * wide].reshape(2, channels, height, wide)
    corner = got_diag[:, :, : height * wide].reshape(4, channels, height, wide)
    above = jnp.concatenate([corner[0, :, -tall:], got_rows[0], corner[1, :, -tall:]], 2)
    middle = jnp.concatenate([side[0], cells, side[1]], 2)
    below = jnp.concatenate([corner[2, :, :tall], got_rows[1], corner[3, :, :tall]], 2)
    got_up = got_up[:, :, : 2 * height2].reshape(2, filters, 2, height2)
    return (
        jnp.concatenate([above, middle, below], 1),
        jnp.concatenate([got_up[0], upstream, got_up[1]], 1),
    )


def greet(count, me, device_of):
    barrier = pltpu.get_barrier_semaphore()

    @pl.loop(1, count)
    def _(step):
        pl.semaphore_signal(
            barrier, inc=1, device_id=device_of(lax.rem(me + step, count)), device_id_type=MESH
        )

    pl.semaphore_wait(barrier, count - 1)


def post(count, me, device_of, source, landing, send_sem, recv_sem):
    def copy_of(step):
        peer = lax.rem(me + step, count)
        return pltpu.make_async_remote_copy(
            src_ref=source(peer),
            dst_ref=landing.at[me],
            send_sem=send_sem.at[step],
            recv_sem=recv_sem.at[me],
            device_id=device_of(peer),
            device_id_type=MESH,
        )

    def arrival(step):
        peer = lax.rem(me + step, count)
        return pltpu.make_async_remote_copy(
            src_ref=source(peer),
            dst_ref=landing.at[peer],
            send_sem=send_sem.at[step],
            recv_sem=recv_sem.at[peer],
            device_id=device_of(peer),
            device_id_type=MESH,
        )

    @pl.loop(1, count)
    def _(step):
        copy_of(step).start()

    def finish():
        @pl.loop(1, count)
        def _(step):
            copy_of(step).wait_send()
            arrival(step).wait_recv()

    return finish


def group(kind):
    rows, strips = lax.axis_size("row"), lax.axis_size(STRIP)
    row, strip = place()
    if kind == "all":
        return (
            rows * strips,
            row * strips + strip,
            lambda i: device_at(lax.div(i, strips), lax.rem(i, strips)),
        )
    if kind == "strips":
        return strips, strip, lambda i: device_at(row, i)
    return rows, row, lambda i: device_at(i, strip)


def gather_kernel(kind, block, out, send_sem, recv_sem):
    count, me, device_of = group(kind)
    greet(count, me, device_of)
    finish = post(count, me, device_of, lambda peer: block, out, send_sem, recv_sem)
    out[me] = block[...]
    finish()


def sems(count):
    return [pltpu.SemaphoreType.DMA((count,)), pltpu.SemaphoreType.DMA((count,))]


def group_size(kind):
    rows, strips = lax.axis_size("row"), lax.axis_size(STRIP)
    return dict(all=rows * strips, strips=strips, rows=rows)[kind]


def gather(block, kind, number):
    count = group_size(kind)
    return pl.pallas_call(
        functools.partial(gather_kernel, kind),
        out_shape=jax.ShapeDtypeStruct((count,) + block.shape, block.dtype),
        in_specs=[VMEM],
        out_specs=VMEM,
        scratch_shapes=sems(count),
        compiler_params=params(number),
    )(block)


def total_of(count, landing):
    return lax.fori_loop(
        1,
        count,
        lambda i, value: value + landing[i].astype(jnp.float32),
        landing[0].astype(jnp.float32),
    )


def scatter_kernel(
    blocks, strip_map, out, maps, landing, send_sem, recv_sem, map_send, map_recv, on_send
):
    rows, me, row_device = group("rows")
    row, strip = place()
    cols, pairs = lax.axis_size("col"), lax.axis_size("pair")
    col, pair = lax.axis_index("col"), lax.axis_index("pair")

    barrier = pltpu.get_barrier_semaphore()
    for step in range(1, rows):
        pl.semaphore_signal(
            barrier, inc=1, device_id=row_device(lax.rem(me + step, rows)), device_id_type=MESH
        )
    for step in range(1, cols):
        pl.semaphore_signal(
            barrier,
            inc=1,
            device_id=device_at(row, lax.rem(col + step, cols) * pairs + pair),
            device_id_type=MESH,
        )
    for step in range(1, pairs):
        pl.semaphore_signal(
            barrier,
            inc=1,
            device_id=device_at(row, col * pairs + lax.rem(pair + step, pairs)),
            device_id_type=MESH,
        )
    pl.semaphore_wait(barrier, rows + cols + pairs - 3)

    def across(step):
        return pltpu.make_async_remote_copy(
            src_ref=strip_map,
            dst_ref=maps.at[strip],
            send_sem=map_send.at[step],
            recv_sem=map_recv.at[strip],
            device_id=device_at(row, lax.rem(col + step, cols) * pairs + pair),
            device_id_type=MESH,
        )

    def onward(source, column, step):
        slot = column * pairs + pair
        return pltpu.make_async_remote_copy(
            src_ref=source,
            dst_ref=maps.at[slot],
            send_sem=on_send.at[column * pairs + step],
            recv_sem=map_recv.at[slot],
            device_id=device_at(row, col * pairs + lax.rem(pair + step, pairs)),
            device_id_type=MESH,
        )

    def arrival(slot):
        return pltpu.make_async_remote_copy(
            src_ref=strip_map,
            dst_ref=maps.at[slot],
            send_sem=map_send.at[0],
            recv_sem=map_recv.at[slot],
            device_id=device_at(row, strip),
            device_id_type=MESH,
        )

    for step in range(1, cols):
        across(step).start()
    finish = post(rows, me, row_device, lambda peer: blocks.at[peer], landing, send_sem, recv_sem)
    for step in range(1, pairs):
        onward(strip_map, col, step).start()
    landing[me] = blocks[me]
    maps[strip] = strip_map[...]
    for step in range(1, cols):
        column = lax.rem(col + step, cols)
        slot = column * pairs + pair
        arrival(slot).wait_recv()
        for other in range(1, pairs):
            onward(maps.at[slot], column, other).start()
    finish()
    out[...] = total_of(rows, landing).astype(out.dtype)
    for step in range(1, cols):
        across(step).wait_send()
    for step in range(cols):
        column = lax.rem(col + step, cols)
        for other in range(1, pairs):
            onward(strip_map, column, other).wait_send()
            arrival(column * pairs + lax.rem(pair + other, pairs)).wait_recv()


def reduce_scatter(blocks, strip_map, number):
    rows, strips = group_size("rows"), group_size("strips")
    return pl.pallas_call(
        scatter_kernel,
        out_shape=(
            jax.ShapeDtypeStruct(blocks.shape[1:], jnp.bfloat16),
            jax.ShapeDtypeStruct((strips,) + strip_map.shape, strip_map.dtype),
        ),
        in_specs=[VMEM] * 2,
        out_specs=(VMEM,) * 2,
        scratch_shapes=[pltpu.VMEM(blocks.shape, blocks.dtype)]
        + sems(rows)
        + sems(strips)
        + [pltpu.SemaphoreType.DMA((strips,))],
        compiler_params=params(number),
    )(blocks, strip_map)


def all_reduce_kernel(blocks, out, landing, part, parts, mine, *semaphores):
    rows, row, row_device = group("rows")
    strips, strip, strip_device = group("strips")
    barrier = pltpu.get_barrier_semaphore()
    for step in range(1, rows):
        pl.semaphore_signal(
            barrier, inc=1, device_id=row_device(lax.rem(row + step, rows)), device_id_type=MESH
        )
    for step in range(1, strips):
        pl.semaphore_signal(
            barrier, inc=1, device_id=strip_device(lax.rem(strip + step, strips)), device_id_type=MESH
        )
    pl.semaphore_wait(barrier, rows + strips - 2)
    one, two, three = semaphores[:2], semaphores[2:4], semaphores[4:]
    finish = post(strips, strip, strip_device, lambda peer: blocks.at[peer], landing, *one)
    landing[strip] = blocks[strip]
    finish()
    total = total_of(strips, landing).astype(part.dtype)
    part[...] = total
    finish = post(rows, row, row_device, lambda peer: part, parts, *two)
    parts[row] = total
    finish()
    total = total_of(rows, parts).astype(part.dtype)
    mine[...] = total
    finish = post(strips, strip, strip_device, lambda peer: mine, out, *three)
    out[strip] = total
    finish()


def all_reduce(blocks, number):
    rows, strips = group_size("rows"), group_size("strips")
    piece, kind = blocks.shape[1:], blocks.dtype
    return pl.pallas_call(
        all_reduce_kernel,
        out_shape=jax.ShapeDtypeStruct(blocks.shape, kind),
        in_specs=[VMEM],
        out_specs=VMEM,
        scratch_shapes=[
            pltpu.VMEM(blocks.shape, kind),
            pltpu.VMEM(piece, kind),
            pltpu.VMEM((rows,) + piece, kind),
            pltpu.VMEM(piece, kind),
        ]
        + sems(strips)
        + sems(rows)
        + sems(strips),
        compiler_params=params(number),
    )(blocks)


def conv_valid(cells, kernel, numbers):
    return lax.conv_general_dilated(
        cells[None], kernel, (1, 1), "VALID", dimension_numbers=numbers, preferred_element_type=jnp.float32
    )[0]


def flip_kernel(kernel):
    return jnp.transpose(kernel[:, ::-1, ::-1, :], (3, 1, 2, 0))


def silu_slope(values):
    sigmoid_value = jax.nn.sigmoid(values)
    return sigmoid_value * (1.0 + values * (1.0 - sigmoid_value))


def tap_grads(gradient, padded, scale, letters, spatial):
    row_count, col_count = (gradient.shape[axis] for axis in spatial)
    taps = []
    for first in range(3):
        for second in range(3):
            window = lax.slice_in_dim(padded, first, first + row_count, axis=spatial[0])
            window = lax.slice_in_dim(window, second, second + col_count, axis=spatial[1])
            taps.append(
                jnp.einsum(letters, gradient, window, preferred_element_type=jnp.float32) * scale
            )
    return jnp.stack(taps, 1)


def local(features_in, filters_one, filters_two, out_grad):
    channels, band, width = features_in.shape
    rows, strips = lax.axis_size("row"), lax.axis_size(STRIP)
    row, strip = place()
    quads = channels * 4
    band2, width2 = band // 4, width // 4
    height2, full2 = band2 * rows, width2 * strips
    filters = filters_two.shape[0]

    features, upstream = halo_exchange(features_in, out_grad, 2, 13, 0)
    pre_one = conv_valid(features, filters_one, ("NCHW", "OHWI", "NCHW"))
    active = jax.nn.silu(pre_one[:, 1:-1])
    near2 = width2 + 6
    pooled = active.reshape(channels, band2, 2, 2, near2, 2, 2).mean(axis=(3, 6))
    at_col = strip * width2 - 3 + jnp.arange(near2)
    inside = ((at_col >= 0) & (at_col < full2))[None, :, None]
    pooled = jnp.transpose(pooled, (1, 3, 0, 2, 4)).reshape(band2, near2, quads)
    pooled = jnp.where(inside, pooled, 0.0).astype(jnp.bfloat16).reshape(band2 * near2, quads)
    spots = band2 * near2
    pooled = jnp.pad(pooled, ((0, -spots % 16), (0, 0)))

    own = gather(pooled, "rows", 1)[:, :spots].reshape(height2, near2, quads)
    pre_two = conv_valid(
        jnp.pad(own, ((1, 1), (0, 0), (0, 0))), filters_two, ("NHWC", "OHWI", "NHWC")
    )
    upstream = jnp.transpose(upstream, (2, 1, 0)).astype(jnp.float32)
    near = (upstream * silu_slope(pre_two)).astype(jnp.bfloat16)

    spread = conv_valid(
        jnp.pad(near, ((1, 1), (0, 0), (0, 0))), flip_kernel(filters_two), ("NHWC", "OHWI", "NHWC")
    )
    channel = jnp.arange(quads)
    low_row = (channel // 2) % 2 == 1
    low_col = channel % 2 == 1
    tall = jnp.pad(spread, ((1, 1), (0, 0), (0, 0)))
    bands = spread.reshape(rows, band2, width2 + 2, quads)
    rim = jnp.where(low_row, tall[0:height2:band2], tall[band2 + 1 : height2 + 2 : band2])
    bands = jnp.concatenate([bands, rim[:, None]], 1)
    edge = jnp.where(low_col, bands[:, :, :1], bands[:, :, -1:])
    bands = jnp.concatenate([bands[:, :, 1:-1], edge], 2).astype(jnp.bfloat16)
    spots = (band2 + 1) * (width2 + 1)
    bands = jnp.pad(bands.reshape(rows, spots, quads), ((0, 0), (0, -spots % 16), (0, 0)))
    strip_map = jnp.concatenate([own[:, 3:-3], near[:, 2:-2]], 2).reshape(height2 * width2, quads + filters)
    grad_pooled, maps = reduce_scatter(bands, strip_map, 2)

    by_part = jnp.arange(quads)
    order = 4 * (by_part % channels) + by_part // channels
    pick = (channel[:, None] == order[None]).astype(jnp.bfloat16)
    parts = jnp.dot(grad_pooled[:spots], pick, preferred_element_type=jnp.float32).astype(jnp.bfloat16)
    parts = parts.reshape(band2 + 1, width2 + 1, 2, 2, channels)
    source = (jnp.arange(width + 2) + 1) // 2
    source = jnp.where(source == 0, 2 * width2 + 1, source - 1)
    place_of = 2 * jnp.arange(width2 + 1)[:, None] + jnp.arange(2)[None]
    expand = (place_of[:, :, None] == source[None, None]).astype(jnp.bfloat16)
    halves = jnp.einsum("uvijc,vjw->uicw", parts, expand, preferred_element_type=jnp.float32)
    halves = halves.reshape(2 * band2 + 2, channels, width + 2)
    halves = jnp.concatenate([halves[-1:], halves[:-1]], 0)
    tall_grad = jnp.repeat(halves, 2, 0)[1:-1] * 0.25
    at_row = row * band - 1 + jnp.arange(band + 2)
    at_col = strip * width - 1 + jnp.arange(width + 2)
    inside = ((at_row >= 0) & (at_row < band * rows))[:, None, None] & (
        (at_col >= 0) & (at_col < width * strips)
    )
    slope = jnp.transpose(silu_slope(pre_one[:, :, 11:-11]), (1, 0, 2))
    grad_ext = jnp.where(inside, tall_grad * slope, 0.0).astype(jnp.bfloat16)

    cells = channels * 9 * channels
    near_in = jnp.transpose(features[:, 1:-1, 12:-12], (1, 0, 2))
    scale = 1.0 / math.sqrt(band * rows * width * strips)
    local_one = tap_grads(grad_ext[1:-1, :, 1:-1], near_in, scale, "how,hcw->oc", (0, 2))
    piece = -(-cells // (strips * 128 * 16)) * 16
    flat = jnp.pad(local_one.reshape(-1).astype(jnp.bfloat16), (0, strips * piece * 128 - cells))
    summed = all_reduce(flat.reshape(strips, piece, 128), 3)
    grad_one = summed.reshape(-1)[:cells].reshape(channels, 3, 3, channels).astype(jnp.float32)

    input_grad = conv_valid(
        jnp.transpose(grad_ext, (1, 0, 2)), flip_kernel(filters_one), ("NCHW", "OHWI", "NCHW")
    ).astype(jnp.bfloat16)

    maps = jnp.transpose(maps.reshape(strips, height2, width2, quads + filters), (1, 0, 2, 3))
    maps = maps.reshape(height2, full2, quads + filters)
    whole = jnp.pad(maps[:, :, :quads], ((1, 1), (1, 1), (0, 0)))
    grad_two = tap_grads(
        maps[:, :, quads:], whole, 1.0 / math.sqrt(height2 * full2), "hwo,hwc->oc", (0, 1)
    )
    return (input_grad, grad_one, grad_two.reshape(filters, 3, 3, quads))


def solution(mesh):
    in_specs = (
        P("grp", "row", ("col", "pair")),
        P(),
        P("row", None, None, None),
        P(("grp", "row"), ("col", "pair"), None),
    )
    out_specs = (
        P("grp", "row", ("col", "pair")),
        P("grp", None, None, None),
        P(("grp", "row"), None, None, None),
    )
    return jax.shard_map(local, mesh=mesh, in_specs=in_specs, out_specs=out_specs, check_vma=False)
```

time: 86.3 us -> 67.2 us (0.78)
  Pallas kernels: 52.1 us -> 35.1 us
  local copies, waits for them, and re-layouts: 15.4 us -> 13.5 us
    pallas_call x2 -> x1, Pallas kernels: 19.5 us -> 7.01 us  [gather(): pl.pallas_call(functools.partial(gather_kernel, kind), out_shape=jax.Shap...]
    pallas_call x2, Pallas kernels: 25.7 us -> 21.1 us  [the longest x1 11.6 us: all_reduce(): pl.pallas_call(all_reduce_kernel, out_shape=jax.ShapeDtypeStruct(blocks.s...]
    reshape x6 -> x4, local copies, waits for them, and re-layouts: 2.05 us -> 0.44 us  [the longest x2 0.22 us: local(): pooled = jnp.transpose(pooled, (1, 3, 0, 2, 4)).reshape(band2, near2, quads)]
    conv_general_dilated x5 -> x4, local copies, waits for them, and re-layouts: 1.66 us -> 0.2 us  [conv_valid(): lax.conv_general_dilated(cells[None], kernel, (1, 1), 'VALID', dimension_...]
    unnamed x52 -> x19, local copies, waits for them, and re-layouts: 3.49 us -> 4.9 us
    slice x8 -> x10, local copies, waits for them, and re-layouts: 2.55 us -> 1.35 us  [the longest x1 1.04 us: halo_exchange(): cells[:, :tall].reshape(channels * tall, width)]
    mul x2, other arithmetic: 1.26 us -> 0.17 us  [the longest x1 0.17 us: local(): active = jax.nn.silu(pre_one[:, 1:-1])]
    another operation x0 -> x3, local copies, waits for them, and re-layouts: none -> 0.95 us  [the longest x2 0.84 us: halo_exchange(): jnp.stack([upstream[:, :2].reshape(filters, 2 * height2), upstream[:, -2:...]
where the time goes in v2:
time: 67.2 us; the launch traced here: 67 us
  Pallas kernels  35.1 us (52%)
  matrix products  14.2 us (21%)
  local copies, waits for them, and re-layouts  13.5 us (20%)
  other arithmetic  2.72 us (4%)
  between operations  1.42 us (2%)
    pallas_call x1, Pallas kernels, all_reduce(): pl.pallas_call(all_reduce_kernel, out_shape=jax.ShapeDtypeStruct(blocks.s...  11.6 us
    pallas_call x1, Pallas kernels, reduce_scatter(): pl.pallas_call(scatter_kernel, out_shape=(jax.ShapeDtypeStruct(blocks.sha...  9.55 us
    conv_general_dilated x4, matrix products, conv_valid(): lax.conv_general_dilated(cells[None], kernel, (1, 1), 'VALID', dimension_...  8.62 us
    pallas_call x1, Pallas kernels, gather(): pl.pallas_call(functools.partial(gather_kernel, kind), out_shape=jax.Shap...  7.01 us
    pallas_call x1, Pallas kernels, halo_exchange(): pl.pallas_call(functools.partial(halo_kernel, rows, strips), out_shape=(j...  6.97 us
    dot_general x18, matrix products, tap_grads(): jnp.einsum(letters, gradient, window, preferred_element_type=jnp.float32)  5.17 us
    unnamed x19, local copies, waits for them, and re-layouts  4.9 us

profile of v2, /device:TPU:0, one launch (start us, length us, event | category | flops | bytes accessed | tf_op | source)
XLA Modules:
  0.0 67.0 jit_solution(2144231368317010714)
XLA Ops:
  0.9 0.7 %slice_bitcast_fusion.3 = (bf16[1,128,16]{1,2,0:T(8,128)(2,1)S(1)}, bf16[1,128,16]{1,2,0:T(8,128)(2,1)S(1)}) fusion(bf16[128,32,8]{0,2,1:T(8,128)(2,1)} %param.7), kind=kLoop, calls=%fused_computation.184 | loop fusion | bytes 16384 | tf_op jit(solution)/shard_map/stack;reshape | solution.py:130
  1.6 0.1 copy.180
  1.8 0.9 %copy.184 = bf16[128,32,8]{0,1,2:T(8,128)(2,1)S(1)} copy(bf16[128,32,8]{0,2,1:T(8,128)(2,1)} %param.7) | data formatting | bytes 131072 | tf_op args[3]
  2.6 1.0 %fusion.149 = (bf16[64,2,128]{2,1,0:T(2,128)(2,1)S(1)}, bf16[64,2,128]{2,1,0:T(2,128)(2,1)S(1)}) fusion(bf16[64,8,128]{2,1,0:T(8,128)(2,1)} %param.4), kind=kLoop, calls=%fused_computation.229 | loop fusion | bytes 131072 | tf_op jit(solution)/shard_map/slice | solution.py:122
  3.7 0.9 %copy.193 = bf16[64,8,128]{2,0,1:T(8,128)(2,1)S(1)} copy(bf16[64,8,128]{2,1,0:T(8,128)(2,1)} %param.4) | data formatting | bytes 262144 | tf_op args[0]
  4.6 1.1 %fusion.148 = (bf16[64,8,13]{2,1,0:T(8,128)(2,1)S(1)}, bf16[64,8,13]{2,1,0:T(8,128)(2,1)S(1)}) fusion(bf16[64,8,128]{2,1,0:T(8,128)(2,1)} %param.4), kind=kLoop, calls=%fused_computation.228 | loop fusion | bytes 53248 | tf_op jit(solution)/shard_map/slice | solution.py:126
  5.7 0.1 reshape.238
  5.8 0.1 reshape.239
  6.0 7.0 %shard_map.67 = (bf16[2,128,128]{2,1,0:T(8,128)(2,1)S(1)}, bf16[2,64,128]{2,1,0:T(8,128)(2,1)S(1)}, bf16[4,64,128]{2,1,0:T(8,128)(2,1)S(1)}, bf16[2,128,128]{2,1,0:T(8,128)(2,1)S(1)}) custom-call(bf16[2,128,128]{2,1,0:T(8,128)(2,1)S(1)} %pad_maximum_fusion.3.edge_rows, bf16[2,64,128]{2,1,0:T(8,128)(2,1)S(1)} %fusion.105.edge_cols, ...), custom_call_target="tpu_custom_call" | custom-call | tf_op jit(solution)/shard_map/pallas_call | solution.py:135
  13.5 0.1 copy.186
  13.7 0.1 copy.262
  13.8 0.1 copy.264
  13.9 0.1 copy.263
  14.0 0.1 copy.265
  14.2 0.2 copy.194
  14.3 0.2 copy.192
  14.5 0.3 fusion.161
  14.7 0.3 maximum_maximum_fusion
  15.0 0.2 slice_bitcast_fusion
  15.2 1.1 %copy.198 = bf16[1,64,12,154]{1,0,3,2:T(2,128)(2,1)S(1)} copy(bf16[1,64,12,154]{3,1,2,0:T(8,128)(2,1)S(1)} %fusion.161) | data formatting | bytes 473088 | tf_op jit(solution)/shard_map/broadcast_in_dim | solution.py:415
  16.3 5.9 %fusion.154 = f32[1,64,10,152]{1,0,3,2:T(1,128)S(1)} fusion(bf16[1,64,12,154]{1,0,3,2:T(2,128)(2,1)S(1)} %copy.198, bf16[64,3,3,64]{3,0,2,1:T(8,128)(2,1)S(1)} %copy-done.1), kind=kOutput, calls=%fused_computation.234 | convolution fusion | flops 112066560 | bytes 699392 | tf_op jit(solution)/shard_map/conv_general_dilated | solution.py:414
  22.2 0.2 divide_multiply_fusion
  22.3 0.6 reduce_sum.9
  23.0 0.2 copy.199
  23.3 0.1 copy.200
  23.5 7.0 %shard_map.68 = bf16[4,80,256]{2,1,0:T(8,128)(2,1)S(1)} custom-call(bf16[80,256]{1,0:T(8,128)(2,1)S(1)} %pad.38.block), custom_call_target="tpu_custom_call" | custom-call | tf_op jit(solution)/shard_map/pallas_call | solution.py:242
  30.7 1.2 %fusion.76 = f32[1,8,36,128]{3,0,2,1:T(1,128)S(1)} fusion(bf16[128,3,3,256]{3,0,2,1:T(8,128)(2,1)S(1)} %copy-done, bf16[1,10,38,256]{3,2,1,0:T(8,128)(2,1)S(1)} %pad_bitcast_fusion), kind=kOutput, calls=%fused_computation.113 | convolution fusion | flops 169869312 | bytes 931840 | tf_op jit(solution)/shard_map/conv_general_dilated | solution.py:414
  32.0 1.0 %fusion.79 = bf16[1,8,34,256]{3,0,2,1:T(2,128)(2,1)S(1)} fusion(bf16[128,3,3,256]{3,0,2,1:T(8,128)(2,1)S(1)} %copy-done, bf16[1,10,36,128]{3,2,1,0:T(8,128)(2,1)S(1)} %pad_bitcast_fusion.1), kind=kOutput, calls=%fused_computation.123 | convolution fusion | flops 160432128 | bytes 821248 | tf_op jit(solution)/shard_map/conv_general_dilated | solution.py:414
  33.3 0.4 slice.229
  33.7 0.4 slice.228
  34.3 0.3 fusion.69
  34.6 0.2 pad_maximum_fusion.1
  34.9 9.5 %shard_map.69 = (bf16[112,256]{1,0:T(8,128)(2,1)S(1)}, bf16[4,256,384]{2,1,0:T(8,128)(2,1)S(1)}) custom-call(bf16[4,112,256]{2,1,0:T(8,128)(2,1)S(1)} %pad.42.blocks, bf16[256,384]{1,0:T(8,128)(2,1)S(1)} %bitcast.340), custom_call_target="tpu_custom_call" | custom-call | tf_op jit(solution)/shard_map/pallas_call | solution.py:347
  44.5 0.2 convolution_convert_fusion
  44.8 0.2 reshape.198
  45.0 0.3 convolution_bitcast_fusion
  45.3 0.2 copy.211
  45.6 0.4 fusion.67
  46.0 0.2 fusion.63
  46.2 0.3 fusion.61
  46.6 0.3 fusion.59
  46.9 0.2 fusion.57
  47.1 0.3 fusion.55
  47.4 0.3 fusion.53
  47.7 0.2 fusion.51
  48.0 0.3 fusion.49
  48.3 0.3 fusion.47
  48.7 0.2 convert_element_type.69
  49.0 11.6 %shard_map.70 = bf16[4,80,128]{2,1,0:T(8,128)(2,1)S(1)} custom-call(bf16[4,80,128]{2,1,0:T(8,128)(2,1)S(1)} %bitcast.342), custom_call_target="tpu_custom_call" | custom-call | tf_op jit(solution)/shard_map/pallas_call | solution.py:395
  60.6 0.1 reshape.207
  60.8 0.6 fusion
  61.5 0.9 %copy.235 = bf16[64,8,128]{2,1,0:T(8,128)(2,1)} copy(bf16[64,8,128]{0,1,2:T(8,128)(2,1)S(1)} %slice_bitcast_fusion.1) | data formatting | bytes 262144
  62.3 0.2 reshape.212
  62.5 0.7 %copy.236 = f32[64,3,3,64]{3,0,2,1:T(8,128)} copy(f32[64,3,3,64]{3,2,1,0:T(4,128)S(1)} %reshape.212) | data formatting | bytes 294912
  63.3 0.3 fusion.3
  63.6 0.3 fusion.6
  63.9 0.3 fusion.9
  64.2 0.3 fusion.12
  64.5 0.3 fusion.15
  64.8 0.3 fusion.18
  65.1 0.3 fusion.21
  65.4 0.3 fusion.24
  65.7 0.3 fusion.27
  66.0 1.0 %copy-done.3 = f32[128,9,256]{2,0,1:T(8,128)} copy-done((f32[128,9,256]{2,0,1:T(8,128)}, f32[128,9,256]{2,0,1:T(8,128)S(1)}, u32[]{:S(2)}) %copy-start.3) | copy-done | bytes 1179672
  (75 shorter events, 2.4 us)
Async XLA Ops:
  0.6 30.0 %copy-start = (bf16[128,3,3,256]{3,0,2,1:T(8,128)(2,1)S(1)}, bf16[128,3,3,256]{3,0,2,1:T(8,128)(2,1)}, u32[]{:S(2)}) copy-start(bf16[128,3,3,256]{3,0,2,1:T(8,128)(2,1)} %param.6) | copy-start | bytes 1769476
  15.0 1.2 %copy-start.1 = (bf16[64,3,3,64]{3,0,2,1:T(8,128)(2,1)S(1)}, bf16[64,3,3,64]{3,0,2,1:T(8,128)(2,1)}, u32[]{:S(2)}) copy-start(bf16[64,3,3,64]{3,0,2,1:T(8,128)(2,1)} %param.5) | copy-start | bytes 221188
  49.0 11.8 %copy-start.2 = (bf16[64,3,3,64]{3,0,2,1:T(8,128)(2,1)S(1)}, bf16[64,3,3,64]{3,0,2,1:T(8,128)(2,1)}, u32[]{:S(2)}) copy-start(bf16[64,3,3,64]{3,0,2,1:T(8,128)(2,1)} %param.5) | copy-start | bytes 221188
  49.0 11.8 %copy-start.4 = (pred[8,17]{0,1:T(8,128)(4,1)S(1)}, pred[8,17]{0,1:T(8,128)(4,1)}, u32[]{:S(2)}) copy-start(pred[8,17]{0,1:T(8,128)(4,1)} %constant.145) | copy-start | bytes 412
  66.0 1.0 %copy-start.3 = (f32[128,9,256]{2,0,1:T(8,128)}, f32[128,9,256]{2,0,1:T(8,128)S(1)}, u32[]{:S(2)}) copy-start(f32[128,9,256]{2,0,1:T(8,128)S(1)} %fusion.27) | copy-start | bytes 3538948

commit v3 on v2

--- a/solution.py
+++ b/solution.py
@@ -31,10 +31,15 @@
 WAYS = [(a, b) for a in (-1, 0, 1) for b in (-1, 0, 1) if (a, b) != (0, 0)]
 
 
-def halo_kernel(
-    rows, strips, edge_rows, edge_cols, edge_up, got_rows, got_cols, got_diag, got_up, send_sem, recv_sem
+def first_kernel(
+    rows, strips, cells, edge_up, kernel, pick_cols, spread_lanes,
+    near, got_up, pre, gathered, shifted, block, send_sem, recv_sem, row_send, row_recv,
 ):
     row, strip = place()
+    band, channels, width = cells.shape
+    band2 = band // 4
+    lanes = [pl.ds(0, width), pl.ds(width, width), pl.ds(2 * width, width)]
+    tops = [pl.ds(0, 2), pl.ds(2, band), pl.ds(band + 2, 2)]
 
     def there(way):
         a, b = row + way[0], strip + way[1]
@@ -42,18 +47,20 @@
 
     barrier = pltpu.get_barrier_semaphore()
     for way in WAYS:
-        @pl.when(there(way))
-        def _(way=way):
-            pl.semaphore_signal(
-                barrier, inc=1, device_id=device_at(row + way[0], strip + way[1]), device_id_type=MESH
-            )
+        if way[1] != 0:
+            @pl.when(there(way))
+            def _(way=way):
+                pl.semaphore_signal(
+                    barrier, inc=1, device_id=device_at(row + way[0], strip + way[1]), device_id_type=MESH
+                )
+    _, _, row_device = group("rows")
+    for step in range(1, rows):
+        pl.semaphore_signal(
+            barrier, inc=1, device_id=row_device(lax.rem(row + step, rows)), device_id_type=MESH
+        )
 
     def landing(way):
-        if way[1] == 0:
-            return got_rows.at[0 if way[0] < 0 else 1]
-        if way[0] == 0:
-            return got_cols.at[0 if way[1] < 0 else 1]
-        return got_diag.at[(0 if way[0] < 0 else 2) + (0 if way[1] < 0 else 1)]
+        return near.at[tops[way[0] + 1], :, lanes[way[1] + 1]]
 
     for way in WAYS:
         @pl.when(jnp.logical_not(there(way)))
@@ -63,17 +70,15 @@
             if way[0] == 0:
                 slot = got_up.at[0 if way[1] < 0 else 1]
                 slot[...] = jnp.zeros(slot.shape, slot.dtype)
+    near[tops[1], :, lanes[1]] = cells[...]
 
     high = 1 + jnp.where(row > 0, 1, 0) + jnp.where(row < rows - 1, 1, 0)
-    across = 1 + jnp.where(strip > 0, 1, 0) + jnp.where(strip < strips - 1, 1, 0)
-    pl.semaphore_wait(barrier, high * across - 1)
+    across = jnp.where(strip > 0, 1, 0) + jnp.where(strip < strips - 1, 1, 0)
+    pl.semaphore_wait(barrier, high * across + rows - 1)
 
     def copy_to(way):
         back = (-way[0], -way[1])
-        if way[1] == 0:
-            source = edge_rows.at[0 if way[0] < 0 else 1]
-        else:
-            source = edge_cols.at[0 if way[1] < 0 else 1]
+        source = cells.at[[pl.ds(0, 2), pl.ds(0, band), pl.ds(band - 2, 2)][way[0] + 1]]
         return pltpu.make_async_remote_copy(
             src_ref=source,
             dst_ref=landing(back),
@@ -94,80 +99,133 @@
             device_id_type=MESH,
         )
 
+    def arrival(way):
+        back = (-way[0], -way[1])
+        return pltpu.make_async_remote_copy(
+            src_ref=landing(way),
+            dst_ref=landing(way),
+            send_sem=send_sem.at[WAYS.index(way)],
+            recv_sem=recv_sem.at[WAYS.index(way)],
+            device_id=device_at(row + back[0], strip + back[1]),
+            device_id_type=MESH,
+        )
+
+    for way in sorted(WAYS, key=lambda w: (abs(w[0]), -abs(w[1]))):
+        @pl.when(there(way))
+        def _(way=way):
+            copy_to(way).start()
+    for way in ((0, -1), (0, 1)):
+        @pl.when(there(way))
+        def _(way=way):
+            upstream_to(way).start()
     for way in WAYS:
         @pl.when(there(way))
         def _(way=way):
-            copy_to(way).start()
-            if way[0] == 0:
-                upstream_to(way).start()
+            arrival(way).wait_recv()
+
+    full = 3 * width
+
+    @pl.loop(0, band + 4)
+    def _(h):
+        here = near[h]
+        wide = here.astype(jnp.float32)
+        shifted[h, pl.ds(0, channels)] = pltpu.roll(wide, 1, 1).astype(jnp.bfloat16)
+        shifted[h, pl.ds(channels, channels)] = here
+        shifted[h, pl.ds(2 * channels, channels)] = pltpu.roll(wide, full - 1, 1).astype(jnp.bfloat16)
+
+    @pl.loop(0, band + 2)
+    def _(h):
+        patches = shifted[pl.ds(h, 3)].reshape(9 * channels, full)
+        pre[h] = jnp.dot(kernel[...], patches, preferred_element_type=jnp.float32)
+
+    def silu(values):
+        return values / (1.0 + jnp.exp(-values))
+
+    contract = (((1,), (1,)), ((), ()))
+    room = pick_cols.shape[0] // 2
+    pooled = []
+    for u in range(band2):
+        total = jnp.zeros((room, 4 * channels), jnp.float32)
+        for i in range(2):
+            at = 1 + 4 * u + 2 * i
+            pair_sum = (silu(pre[at]) + silu(pre[at + 1])) * 0.25
+            upper = pair_sum.astype(jnp.bfloat16)
+            lower = (pair_sum - upper.astype(jnp.float32)).astype(jnp.bfloat16)
+            mean = lax.dot_general(pick_cols[...], upper, contract, preferred_element_type=jnp.float32)
+            mean += lax.dot_general(pick_cols[...], lower, contract, preferred_element_type=jnp.float32)
+            mean = mean.astype(jnp.bfloat16)
+            for j in range(2):
+                total += jnp.dot(
+                    mean[j * room : (j + 1) * room],
+                    spread_lanes[2 * i + j],
+                    preferred_element_type=jnp.float32,
+                )
+        pooled.append(total)
+    pooled = jnp.concatenate(pooled, 0).astype(jnp.bfloat16)
+    block[...] = pooled
+    finish = post(rows, row, row_device, lambda peer: block, gathered, row_send, row_recv)
+    gathered[row] = pooled
     for way in WAYS:
         @pl.when(there(way))
         def _(way=way):
-            back = (-way[0], -way[1])
             copy_to(way).wait_send()
-            copy_to(back).wait_recv()
             if way[0] == 0:
                 upstream_to(way).wait_send()
-                upstream_to(back).wait_recv()
-
-
-def pad_lanes(cells):
-    return jnp.pad(cells, [(0, 0)] * (cells.ndim - 1) + [(0, -cells.shape[-1] % 128)])
-
-
-def halo_exchange(cells, upstream, tall, wide, number):
-    channels, height, width = cells.shape
-    filters, count, height2 = upstream.shape
-    edge_rows = jnp.stack(
-        [cells[:, :tall].reshape(channels * tall, width), cells[:, -tall:].reshape(channels * tall, width)]
-    )
-    edge_cols = pad_lanes(
-        jnp.stack(
-            [cells[:, :, :wide].reshape(channels, height * wide), cells[:, :, -wide:].reshape(channels, height * wide)]
-        )
-    )
-    edge_up = pad_lanes(
-        jnp.stack(
-            [upstream[:, :2].reshape(filters, 2 * height2), upstream[:, -2:].reshape(filters, 2 * height2)]
-        )
-    )
+                upstream_to((-way[0], -way[1])).wait_recv()
+    finish()
+
+
+def first_layer(features_in, upstream, filters_one, number):
+    channels, band, width = features_in.shape
     rows, strips = lax.axis_size("row"), lax.axis_size(STRIP)
-    got_rows, got_cols, got_diag, got_up = pl.pallas_call(
-        functools.partial(halo_kernel, rows, strips),
+    strip = lax.axis_index(STRIP)
+    band2, width2 = band // 4, width // 4
+    quads = 4 * channels
+    near2 = width2 + 6
+    room = -(-near2 // 16) * 16
+    if (band2 * (-(-near2 // 8) * 8)) % 16 == 0:
+        room = -(-near2 // 8) * 8
+    height2, _, filters = upstream.shape
+    cells = jnp.transpose(features_in, (1, 0, 2))
+    edge_up = jnp.stack(
+        [upstream[:, :2].reshape(2 * height2, filters), upstream[:, -2:].reshape(2 * height2, filters)]
+    )
+    v = jnp.arange(room)
+    start = width + 4 * (v - 3)[None, :, None] + 2 * jnp.arange(2)[:, None, None]
+    lane = jnp.arange(3 * width)[None, None, :]
+    at_col = strip * width2 - 3 + v
+    inside = (v < near2) & (at_col >= 0) & (at_col < width2 * strips)
+    pick_cols = ((lane == start) | (lane == start + 1)) & inside[None, :, None]
+    pick_cols = pick_cols.astype(jnp.bfloat16).reshape(2 * room, 3 * width)
+    target = 4 * jnp.arange(channels)[None, :, None] + jnp.arange(4)[:, None, None]
+    spread_lanes = (jnp.arange(quads)[None, None] == target).astype(jnp.bfloat16)
+    near, got_up, pre, gathered = pl.pallas_call(
+        functools.partial(first_kernel, rows, strips),
         out_shape=(
-            jax.ShapeDtypeStruct(edge_rows.shape, cells.dtype),
-            jax.ShapeDtypeStruct(edge_cols.shape, cells.dtype),
-            jax.ShapeDtypeStruct((4,) + edge_cols.shape[1:], cells.dtype),
-            jax.ShapeDtypeStruct(edge_up.shape, cells.dtype),
+            jax.ShapeDtypeStruct((band + 4, channels, 3 * width), jnp.bfloat16),
+            jax.ShapeDtypeStruct(edge_up.shape, jnp.bfloat16),
+            jax.ShapeDtypeStruct((band + 2, channels, 3 * width), jnp.float32),
+            jax.ShapeDtypeStruct((rows, band2 * room, quads), jnp.bfloat16),
         ),
-        in_specs=[VMEM] * 3,
+        in_specs=[VMEM] * 5,
         out_specs=(VMEM,) * 4,
-        scratch_shapes=[pltpu.SemaphoreType.DMA((10,)), pltpu.SemaphoreType.DMA((10,))],
+        scratch_shapes=[
+            pltpu.VMEM((band + 4, 3 * channels, 3 * width), jnp.bfloat16),
+            pltpu.VMEM((band2 * room, quads), jnp.bfloat16),
+        ]
+        + sems(10)
+        + sems(rows),
         compiler_params=params(number),
-    )(edge_rows, edge_cols, edge_up)
-    got_rows = got_rows.reshape(2, channels, tall, width)
-    side = got_cols[:, :, : height * wide].reshape(2, channels, height, wide)
-    corner = got_diag[:, :, : height * wide].reshape(4, channels, height, wide)
-    above = jnp.concatenate([corner[0, :, -tall:], got_rows[0], corner[1, :, -tall:]], 2)
-    middle = jnp.concatenate([side[0], cells, side[1]], 2)
-    below = jnp.concatenate([corner[2, :, :tall], got_rows[1], corner[3, :, :tall]], 2)
-    got_up = got_up[:, :, : 2 * height2].reshape(2, filters, 2, height2)
+    )(cells, edge_up, filters_one.reshape(channels, 9 * channels), pick_cols, spread_lanes)
+    own = gathered.reshape(rows * band2, room, quads)[:, :near2]
+    got_up = got_up.reshape(2, height2, 2, filters)
+    inner = slice(width - 1, 2 * width + 1)
     return (
-        jnp.concatenate([above, middle, below], 1),
+        near[1:-1, :, inner],
+        pre[:, :, inner],
+        own,
         jnp.concatenate([got_up[0], upstream, got_up[1]], 1),
     )
-
-
-def greet(count, me, device_of):
-    barrier = pltpu.get_barrier_semaphore()
-
-    @pl.loop(1, count)
-    def _(step):
-        pl.semaphore_signal(
-            barrier, inc=1, device_id=device_of(lax.rem(me + step, count)), device_id_type=MESH
-        )
-
-    pl.semaphore_wait(barrier, count - 1)
 
 
 def post(count, me, device_of, source, landing, send_sem, recv_sem):
@@ -220,14 +278,6 @@
     return rows, row, lambda i: device_at(i, strip)
 
 
-def gather_kernel(kind, block, out, send_sem, recv_sem):
-    count, me, device_of = group(kind)
-    greet(count, me, device_of)
-    finish = post(count, me, device_of, lambda peer: block, out, send_sem, recv_sem)
-    out[me] = block[...]
-    finish()
-
-
 def sems(count):
     return [pltpu.SemaphoreType.DMA((count,)), pltpu.SemaphoreType.DMA((count,))]
 
@@ -235,18 +285,6 @@
 def group_size(kind):
     rows, strips = lax.axis_size("row"), lax.axis_size(STRIP)
     return dict(all=rows * strips, strips=strips, rows=rows)[kind]
-
-
-def gather(block, kind, number):
-    count = group_size(kind)
-    return pl.pallas_call(
-        functools.partial(gather_kernel, kind),
-        out_shape=jax.ShapeDtypeStruct((count,) + block.shape, block.dtype),
-        in_specs=[VMEM],
-        out_specs=VMEM,
-        scratch_shapes=sems(count),
-        compiler_params=params(number),
-    )(block)
 
 
 def total_of(count, landing):
@@ -447,24 +485,13 @@
     height2, full2 = band2 * rows, width2 * strips
     filters = filters_two.shape[0]
 
-    features, upstream = halo_exchange(features_in, out_grad, 2, 13, 0)
-    pre_one = conv_valid(features, filters_one, ("NCHW", "OHWI", "NCHW"))
-    active = jax.nn.silu(pre_one[:, 1:-1])
-    near2 = width2 + 6
-    pooled = active.reshape(channels, band2, 2, 2, near2, 2, 2).mean(axis=(3, 6))
-    at_col = strip * width2 - 3 + jnp.arange(near2)
-    inside = ((at_col >= 0) & (at_col < full2))[None, :, None]
-    pooled = jnp.transpose(pooled, (1, 3, 0, 2, 4)).reshape(band2, near2, quads)
-    pooled = jnp.where(inside, pooled, 0.0).astype(jnp.bfloat16).reshape(band2 * near2, quads)
-    spots = band2 * near2
-    pooled = jnp.pad(pooled, ((0, -spots % 16), (0, 0)))
-
-    own = gather(pooled, "rows", 1)[:, :spots].reshape(height2, near2, quads)
+    near_in, pre_one, own, upstream = first_layer(
+        features_in, jnp.transpose(out_grad, (2, 1, 0)), filters_one, 0
+    )
     pre_two = conv_valid(
         jnp.pad(own, ((1, 1), (0, 0), (0, 0))), filters_two, ("NHWC", "OHWI", "NHWC")
     )
-    upstream = jnp.transpose(upstream, (2, 1, 0)).astype(jnp.float32)
-    near = (upstream * silu_slope(pre_two)).astype(jnp.bfloat16)
+    near = (upstream.astype(jnp.float32) * silu_slope(pre_two)).astype(jnp.bfloat16)
 
     spread = conv_valid(
         jnp.pad(near, ((1, 1), (0, 0), (0, 0))), flip_kernel(filters_two), ("NHWC", "OHWI", "NHWC")
@@ -501,11 +528,9 @@
     inside = ((at_row >= 0) & (at_row < band * rows))[:, None, None] & (
         (at_col >= 0) & (at_col < width * strips)
     )
-    slope = jnp.transpose(silu_slope(pre_one[:, :, 11:-11]), (1, 0, 2))
-    grad_ext = jnp.where(inside, tall_grad * slope, 0.0).astype(jnp.bfloat16)
+    grad_ext = jnp.where(inside, tall_grad * silu_slope(pre_one), 0.0).astype(jnp.bfloat16)
 
     cells = channels * 9 * channels
-    near_in = jnp.transpose(features[:, 1:-1, 12:-12], (1, 0, 2))
     scale = 1.0 / math.sqrt(band * rows * width * strips)
     local_one = tap_grads(grad_ext[1:-1, :, 1:-1], near_in, scale, "how,hcw->oc", (0, 2))
     piece = -(-cells // (strips * 128 * 16)) * 16

time: 67.2 us -> 59 us (0.88)
  matrix products: 14.2 us -> 8.16 us
  local copies, waits for them, and re-layouts: 13.5 us -> 9.38 us
  Pallas kernels: 35.1 us -> 38.6 us
  other arithmetic: 2.72 us -> 1.4 us
    conv_general_dilated x4 -> x3, matrix products: 8.62 us -> 2.73 us  [conv_valid(): lax.conv_general_dilated(cells[None], kernel, (1, 1), 'VALID', dimension_...]
    pallas_call x2 -> x1, Pallas kernels: 14 us -> 18.1 us  [first_layer(): pl.pallas_call(functools.partial(first_kernel, rows, strips), out_shape=(...]
    slice x11 -> x2, local copies, waits for them, and re-layouts: 2.68 us -> 0.01 us  [the longest x1 0.01 us: first_layer(): upstream[:, :2].reshape(2 * height2, filters)]
    unnamed x19, local copies, waits for them, and re-layouts: 4.9 us -> 6.36 us
    another operation x4 -> x0, local copies, waits for them, and re-layouts: 1.1 us -> none  [the longest x2 0.84 us: halo_exchange(): jnp.stack([upstream[:, :2].reshape(filters, 2 * height2), upstream[:, -2:...]
    broadcast_in_dim x4 -> x3, local copies, waits for them, and re-layouts: 1.15 us -> 0.1 us  [conv_valid(): cells[None]]
    pallas_call x1, Pallas kernels: 9.55 us -> 8.7 us  [reduce_scatter(): pl.pallas_call(scatter_kernel, out_shape=(jax.ShapeDtypeStruct(blocks.sha...]
where the time goes in v3:
time: 59 us; the launch traced here: 58.8 us
  Pallas kernels  38.6 us (65%)
  local copies, waits for them, and re-layouts  9.38 us (16%)
  matrix products  8.16 us (14%)
  other arithmetic  1.4 us (2%)
  between operations  1.28 us (2%)
    pallas_call x1, Pallas kernels, first_layer(): pl.pallas_call(functools.partial(first_kernel, rows, strips), out_shape=(...  18.1 us
    pallas_call x1, Pallas kernels, all_reduce(): pl.pallas_call(all_reduce_kernel, out_shape=jax.ShapeDtypeStruct(blocks.s...  11.7 us
    pallas_call x1, Pallas kernels, reduce_scatter(): pl.pallas_call(scatter_kernel, out_shape=(jax.ShapeDtypeStruct(blocks.sha...  8.7 us
    unnamed x19, local copies, waits for them, and re-layouts  6.36 us
    dot_general x18, matrix products, tap_grads(): jnp.einsum(letters, gradient, window, preferred_element_type=jnp.float32)  5 us
    conv_general_dilated x3, matrix products, conv_valid(): lax.conv_general_dilated(cells[None], kernel, (1, 1), 'VALID', dimension_...  2.73 us

profile of v3, /device:TPU:0, one launch (start us, length us, event | category | flops | bytes accessed | tf_op | source)
XLA Modules:
  0.0 58.8 jit_solution(9006380524290178924)
XLA Ops:
  0.6 0.0 copy-start
  0.7 0.1 and.120
  0.8 0.1 add.204
  0.9 0.1 add.205
  1.0 0.1 add.206
  1.1 0.1 broadcast_and_fusion
  1.2 0.1 fusion.101.pick_cols
  1.3 0.9 %copy.111 = bf16[128,32,8]{0,1,2:T(8,128)(2,1)S(1)} copy(bf16[128,32,8]{0,2,1:T(8,128)(2,1)} %param.7) | data formatting | bytes 131072 | tf_op args[3]
  2.2 0.1 fusion.78.spread_lanes
  2.3 0.9 %copy.110 = bf16[64,8,128]{2,0,1:T(8,128)(2,1)S(1)} copy(bf16[64,8,128]{2,1,0:T(8,128)(2,1)} %param.4) | data formatting | bytes 262144 | tf_op args[0]
  3.2 1.0 %copy.57 = bf16[64,3,3,64]{0,3,2,1:T(8,128)(2,1)S(1)} copy(bf16[64,3,3,64]{3,0,2,1:T(8,128)(2,1)} %param.5) | data formatting | bytes 147456 | tf_op args[1]
  4.3 0.1 copy.58.kernel
  4.4 18.1 %shard_map.67 = (bf16[12,64,384]{2,1,0:T(8,128)(2,1)S(1)}, bf16[2,16,128]{2,1,0:T(8,128)(2,1)S(1)}, f32[10,64,384]{2,1,0:T(8,128)S(1)}, bf16[4,80,256]{2,1,0:T(8,128)(2,1)S(1)}) custom-call(bf16[8,64,128]{2,1,0:T(8,128)(2,1)S(1)} %bitcast.321, bf16[2,16,128]{2,1,0:T(8,128)(2,1)S(1)} %pad_maximum_fusion.4.edge_up, bf16[64,576]{1,0:T(8,128)(2,1)S(1)} %copy.58.kernel, ...), custom_call_target="tpu_custom_call" | custom-call | tf_op jit(solution)/shard_map/pallas_call | solution.py:202
  22.6 1.2 %fusion.76 = f32[1,8,36,128]{3,0,2,1:T(1,128)S(1)} fusion(bf16[128,3,3,256]{3,0,2,1:T(8,128)(2,1)S(1)} %copy-done, bf16[1,10,38,256]{3,2,1,0:T(8,128)(2,1)S(1)} %pad_bitcast_fusion), kind=kOutput, calls=%fused_computation.111 | convolution fusion | flops 169869312 | bytes 931840 | tf_op jit(solution)/shard_map/conv_general_dilated | solution.py:452
  23.8 0.1 fusion.88
  24.0 1.0 %fusion.80 = bf16[1,8,34,256]{3,0,2,1:T(2,128)(2,1)S(1)} fusion(bf16[128,3,3,256]{3,0,2,1:T(8,128)(2,1)S(1)} %copy-done, bf16[1,10,36,128]{3,2,1,0:T(8,128)(2,1)S(1)} %pad_bitcast_fusion.1), kind=kOutput, calls=%fused_computation.122 | convolution fusion | flops 160432128 | bytes 821248 | tf_op jit(solution)/shard_map/conv_general_dilated | solution.py:452
  25.1 0.1 copy.98
  25.2 0.1 pad.26
  25.3 0.4 slice.165
  25.7 0.4 slice.164
  26.1 0.1 broadcast_in_dim.58
  26.3 0.3 fusion.69
  26.5 0.2 pad_maximum_fusion.1
  26.7 0.1 copy.66
  26.9 8.7 %shard_map.68 = (bf16[112,256]{1,0:T(8,128)(2,1)S(1)}, bf16[4,256,384]{2,1,0:T(8,128)(2,1)S(1)}) custom-call(bf16[4,112,256]{2,1,0:T(8,128)(2,1)S(1)} %pad.27.blocks, bf16[256,384]{1,0:T(8,128)(2,1)S(1)} %bitcast.318), custom_call_target="tpu_custom_call" | custom-call | tf_op jit(solution)/shard_map/pallas_call | solution.py:385
  35.6 0.2 convolution_convert_fusion
  35.8 0.1 copy.74
  35.9 0.2 reshape.278
  36.1 0.3 convolution_bitcast_fusion
  36.4 0.1 broadcast_in_dim.61
  36.5 0.4 fusion.67
  36.9 0.0 copy-start.1
  36.9 0.3 fusion.63
  37.2 0.2 fusion.61
  37.4 0.3 fusion.59
  37.7 0.3 fusion.57
  38.0 0.2 fusion.55
  38.2 0.3 fusion.53
  38.5 0.3 fusion.51
  38.8 0.2 fusion.49
  39.0 0.3 fusion.47
  39.3 0.0 copy-start.2
  39.3 0.1 copy.73
  39.4 0.2 convert_element_type.63
  39.6 11.7 %shard_map.69 = bf16[4,80,128]{2,1,0:T(8,128)(2,1)S(1)} custom-call(bf16[4,80,128]{2,1,0:T(8,128)(2,1)S(1)} %bitcast.322), custom_call_target="tpu_custom_call" | custom-call | tf_op jit(solution)/shard_map/pallas_call | solution.py:433
  51.4 0.2 reshape.292
  51.6 0.7 %copy.85 = f32[64,3,3,64]{3,0,2,1:T(8,128)} copy(f32[64,3,3,64]{3,2,1,0:T(4,128)S(1)} %reshape.292) | data formatting | bytes 294912
  52.3 0.3 copy.100
  52.6 0.0 copy-start.5
  52.6 0.1 pad.30.clone
  52.7 0.1 reshape.287
  52.9 0.6 %copy-done.3 = bf16[64,3,3,64]{3,0,2,1:T(8,128)(2,1)S(1)} copy-done((bf16[64,3,3,64]{3,0,2,1:T(8,128)(2,1)S(1)}, bf16[64,3,3,64]{3,0,2,1:T(8,128)(2,1)}, u32[]{:S(2)}) %copy-start.3) | copy-done | bytes 73752
  53.5 0.6 fusion
  54.1 0.9 %copy.84 = bf16[64,8,128]{2,1,0:T(8,128)(2,1)} copy(bf16[64,8,128]{0,1,2:T(8,128)(2,1)S(1)} %slice_bitcast_fusion) | data formatting | bytes 262144
  55.0 0.3 fusion.3
  55.3 0.3 fusion.6
  55.6 0.3 fusion.9
  55.9 0.3 fusion.12
  56.2 0.3 fusion.15
  56.5 0.3 fusion.18
  56.9 0.3 fusion.21
  57.2 0.3 fusion.24
  57.5 0.3 fusion.27
  57.8 1.0 %copy-done.4 = f32[128,9,256]{2,0,1:T(8,128)} copy-done((f32[128,9,256]{2,0,1:T(8,128)}, f32[128,9,256]{2,0,1:T(8,128)S(1)}, u32[]{:S(2)}) %copy-start.4) | copy-done | bytes 1179672
  (47 shorter events, 0.6 us)
Async XLA Ops:
  0.6 22.0 %copy-start = (bf16[128,3,3,256]{3,0,2,1:T(8,128)(2,1)S(1)}, bf16[128,3,3,256]{3,0,2,1:T(8,128)(2,1)}, u32[]{:S(2)}) copy-start(bf16[128,3,3,256]{3,0,2,1:T(8,128)(2,1)} %param.6) | copy-start | bytes 1769476
  36.9 2.1 %copy-start.1 = (bf16[10,64,130]{2,1,0:T(8,128)(2,1)}, bf16[10,64,130]{2,1,0:T(8,128)(2,1)S(1)}, u32[]{:S(2)}) copy-start(bf16[10,64,130]{2,1,0:T(8,128)(2,1)S(1)} %fusion.67) | copy-start | bytes 499204
  39.3 13.0 %copy-start.2 = (bf16[10,64,130]{2,1,0:T(8,128)(2,1)S(1)}, bf16[10,64,130]{2,1,0:T(8,128)(2,1)}, u32[]{:S(2)}) copy-start(bf16[10,64,130]{2,1,0:T(8,128)(2,1)} %copy-done.1) | copy-start | bytes 499204
  52.6 0.9 %copy-start.3 = (bf16[64,3,3,64]{3,0,2,1:T(8,128)(2,1)S(1)}, bf16[64,3,3,64]{3,0,2,1:T(8,128)(2,1)}, u32[]{:S(2)}) copy-start(bf16[64,3,3,64]{3,0,2,1:T(8,128)(2,1)} %param.5) | copy-start | bytes 221188
  52.6 0.9 %copy-start.5 = (pred[8,17]{0,1:T(8,128)(4,1)S(1)}, pred[8,17]{0,1:T(8,128)(4,1)}, u32[]{:S(2)}) copy-start(pred[8,17]{0,1:T(8,128)(4,1)} %constant.144) | copy-start | bytes 412
  57.8 1.0 %copy-start.4 = (f32[128,9,256]{2,0,1:T(8,128)}, f32[128,9,256]{2,0,1:T(8,128)S(1)}, u32[]{:S(2)}) copy-start(f32[128,9,256]{2,0,1:T(8,128)S(1)} %fusion.27) | copy-start | bytes 3538948

commit v4 on v3

--- a/solution.py
+++ b/solution.py
@@ -33,7 +33,7 @@
 
 def first_kernel(
     rows, strips, cells, edge_up, kernel, pick_cols, spread_lanes,
-    near, got_up, pre, gathered, shifted, block, send_sem, recv_sem, row_send, row_recv,
+    got_up, pre, gathered, shifted, near, block, send_sem, recv_sem, row_send, row_recv,
 ):
     row, strip = place()
     band, channels, width = cells.shape
@@ -199,18 +199,18 @@
     pick_cols = pick_cols.astype(jnp.bfloat16).reshape(2 * room, 3 * width)
     target = 4 * jnp.arange(channels)[None, :, None] + jnp.arange(4)[:, None, None]
     spread_lanes = (jnp.arange(quads)[None, None] == target).astype(jnp.bfloat16)
-    near, got_up, pre, gathered = pl.pallas_call(
+    got_up, pre, gathered, shifted = pl.pallas_call(
         functools.partial(first_kernel, rows, strips),
         out_shape=(
-            jax.ShapeDtypeStruct((band + 4, channels, 3 * width), jnp.bfloat16),
             jax.ShapeDtypeStruct(edge_up.shape, jnp.bfloat16),
             jax.ShapeDtypeStruct((band + 2, channels, 3 * width), jnp.float32),
             jax.ShapeDtypeStruct((rows, band2 * room, quads), jnp.bfloat16),
+            jax.ShapeDtypeStruct((band + 4, 3 * channels, 3 * width), jnp.bfloat16),
         ),
         in_specs=[VMEM] * 5,
         out_specs=(VMEM,) * 4,
         scratch_shapes=[
-            pltpu.VMEM((band + 4, 3 * channels, 3 * width), jnp.bfloat16),
+            pltpu.VMEM((band + 4, channels, 3 * width), jnp.bfloat16),
             pltpu.VMEM((band2 * room, quads), jnp.bfloat16),
         ]
         + sems(10)
@@ -221,7 +221,7 @@
     got_up = got_up.reshape(2, height2, 2, filters)
     inner = slice(width - 1, 2 * width + 1)
     return (
-        near[1:-1, :, inner],
+        shifted,
         pre[:, :, inner],
         own,
         jnp.concatenate([got_up[0], upstream, got_up[1]], 1),
@@ -398,7 +398,9 @@
     )(blocks, strip_map)
 
 
-def all_reduce_kernel(blocks, out, landing, part, parts, mine, *semaphores):
+def last_kernel(
+    scale, shifted, gradient, grad_two_in, whole, out, taps, blocks, landing, part, parts, mine, *semaphores
+):
     rows, row, row_device = group("rows")
     strips, strip, strip_device = group("strips")
     barrier = pltpu.get_barrier_semaphore()
@@ -410,33 +412,77 @@
         pl.semaphore_signal(
             barrier, inc=1, device_id=strip_device(lax.rem(strip + step, strips)), device_id_type=MESH
         )
+    band, channels, width = gradient.shape
+    steps, _, spots = grad_two_in.shape
+    full2 = whole.shape[1] - 2
+    chunk = spots // full2
+    quads = whole.shape[2]
+
+    def one_row(h, total):
+        patches = shifted[pl.ds(h + 1, 3), :, pl.ds(width, width)].reshape(9 * channels, width)
+        return total + lax.dot_general(
+            gradient[h], patches, (((1,), (1,)), ((), ())), preferred_element_type=jnp.float32
+        )
+
+    total = lax.fori_loop(0, band, one_row, jnp.zeros((channels, 9 * channels), jnp.float32))
+    height = channels // strips
+    for peer in range(strips):
+        blocks[peer] = total[peer * height : (peer + 1) * height].astype(blocks.dtype)
+
+    def tap(index):
+        first, second = divmod(index, 3)
+
+        def product(step):
+            window = whole[pl.ds(step * chunk + first, chunk), pl.ds(second, full2)]
+            return scale * jnp.dot(
+                grad_two_in[step], window.reshape(spots, quads), preferred_element_type=jnp.float32
+            )
+
+        taps[index] = product(0)
+        if steps > 1:
+            @pl.loop(1, steps)
+            def _(step):
+                taps[index] += product(step)
+
     pl.semaphore_wait(barrier, rows + strips - 2)
     one, two, three = semaphores[:2], semaphores[2:4], semaphores[4:]
     finish = post(strips, strip, strip_device, lambda peer: blocks.at[peer], landing, *one)
     landing[strip] = blocks[strip]
+    for index in range(3):
+        tap(index)
     finish()
     total = total_of(strips, landing).astype(part.dtype)
     part[...] = total
     finish = post(rows, row, row_device, lambda peer: part, parts, *two)
     parts[row] = total
+    for index in range(3, 6):
+        tap(index)
     finish()
     total = total_of(rows, parts).astype(part.dtype)
     mine[...] = total
     finish = post(strips, strip, strip_device, lambda peer: mine, out, *three)
     out[strip] = total
+    for index in range(6, 9):
+        tap(index)
     finish()
 
 
-def all_reduce(blocks, number):
+def last_layer(shifted, gradient, grad_two_in, whole, scale, number):
     rows, strips = group_size("rows"), group_size("strips")
-    piece, kind = blocks.shape[1:], blocks.dtype
+    channels = gradient.shape[1]
+    kind = jnp.bfloat16
+    piece = (channels // strips, 9 * channels)
     return pl.pallas_call(
-        all_reduce_kernel,
-        out_shape=jax.ShapeDtypeStruct(blocks.shape, kind),
-        in_specs=[VMEM],
-        out_specs=VMEM,
+        functools.partial(last_kernel, scale),
+        out_shape=(
+            jax.ShapeDtypeStruct((strips,) + piece, kind),
+            jax.ShapeDtypeStruct((9, grad_two_in.shape[1], whole.shape[2]), jnp.float32),
+        ),
+        in_specs=[VMEM] * 4,
+        out_specs=(VMEM,) * 2,
         scratch_shapes=[
-            pltpu.VMEM(blocks.shape, kind),
+            pltpu.VMEM((strips,) + piece, kind),
+            pltpu.VMEM((strips,) + piece, kind),
             pltpu.VMEM(piece, kind),
             pltpu.VMEM((rows,) + piece, kind),
             pltpu.VMEM(piece, kind),
@@ -445,7 +491,7 @@
         + sems(rows)
         + sems(strips),
         compiler_params=params(number),
-    )(blocks)
+    )(shifted, gradient, grad_two_in, whole)
 
 
 def conv_valid(cells, kernel, numbers):
@@ -461,19 +507,6 @@
 def silu_slope(values):
     sigmoid_value = jax.nn.sigmoid(values)
     return sigmoid_value * (1.0 + values * (1.0 - sigmoid_value))
-
-
-def tap_grads(gradient, padded, scale, letters, spatial):
-    row_count, col_count = (gradient.shape[axis] for axis in spatial)
-    taps = []
-    for first in range(3):
-        for second in range(3):
-            window = lax.slice_in_dim(padded, first, first + row_count, axis=spatial[0])
-            window = lax.slice_in_dim(window, second, second + col_count, axis=spatial[1])
-            taps.append(
-                jnp.einsum(letters, gradient, window, preferred_element_type=jnp.float32) * scale
-            )
-    return jnp.stack(taps, 1)
 
 
 def local(features_in, filters_one, filters_two, out_grad):
@@ -485,7 +518,7 @@
     height2, full2 = band2 * rows, width2 * strips
     filters = filters_two.shape[0]
 
-    near_in, pre_one, own, upstream = first_layer(
+    shifted, pre_one, own, upstream = first_layer(
         features_in, jnp.transpose(out_grad, (2, 1, 0)), filters_one, 0
     )
     pre_two = conv_valid(
@@ -530,25 +563,28 @@
     )
     grad_ext = jnp.where(inside, tall_grad * silu_slope(pre_one), 0.0).astype(jnp.bfloat16)
 
-    cells = channels * 9 * channels
+    maps = jnp.transpose(maps.reshape(strips, height2, width2, quads + filters), (1, 0, 2, 3))
+    maps = maps.reshape(height2, full2, quads + filters)
+    whole = jnp.pad(maps[:, :, :quads], ((1, 1), (1, 1), (0, 0)))
+    chunk = max(1, 1024 // full2)
+    grad_two_in = maps[:, :, quads:].reshape(height2 // chunk, chunk * full2, filters)
+    summed, taps = last_layer(
+        shifted,
+        grad_ext[1:-1, :, 1:-1],
+        jnp.transpose(grad_two_in, (0, 2, 1)),
+        whole,
+        1.0 / math.sqrt(height2 * full2),
+        3,
+    )
     scale = 1.0 / math.sqrt(band * rows * width * strips)
-    local_one = tap_grads(grad_ext[1:-1, :, 1:-1], near_in, scale, "how,hcw->oc", (0, 2))
-    piece = -(-cells // (strips * 128 * 16)) * 16
-    flat = jnp.pad(local_one.reshape(-1).astype(jnp.bfloat16), (0, strips * piece * 128 - cells))
-    summed = all_reduce(flat.reshape(strips, piece, 128), 3)
-    grad_one = summed.reshape(-1)[:cells].reshape(channels, 3, 3, channels).astype(jnp.float32)
+    grad_one = summed.astype(jnp.float32).reshape(channels, 3, 3, channels) * scale
+    grad_two = jnp.transpose(taps, (1, 0, 2)).reshape(filters, 3, 3, quads)
 
     input_grad = conv_valid(
         jnp.transpose(grad_ext, (1, 0, 2)), flip_kernel(filters_one), ("NCHW", "OHWI", "NCHW")
     ).astype(jnp.bfloat16)
 
-    maps = jnp.transpose(maps.reshape(strips, height2, width2, quads + filters), (1, 0, 2, 3))
-    maps = maps.reshape(height2, full2, quads + filters)
-    whole = jnp.pad(maps[:, :, :quads], ((1, 1), (1, 1), (0, 0)))
-    grad_two = tap_grads(
-        maps[:, :, quads:], whole, 1.0 / math.sqrt(height2 * full2), "hwo,hwc->oc", (0, 1)
-    )
-    return (input_grad, grad_one, grad_two.reshape(filters, 3, 3, quads))
+    return (input_grad, grad_one, grad_two)
 
 
 def solution(mesh):

time: 59 us -> 60.6 us (1.027)
  matrix products: 8.16 us -> 3.16 us
  local copies, waits for them, and re-layouts: 9.38 us -> 14.1 us
  other arithmetic: 1.4 us -> 2.82 us
    dot_general x18 -> x0, matrix products: 5 us -> none  [tap_grads(): jnp.einsum(letters, gradient, window, preferred_element_type=jnp.float32)]
    unnamed x19 -> x24, local copies, waits for them, and re-layouts: 6.36 us -> 8.37 us
    convert_element_type x1, other arithmetic: 0.35 us -> 1.76 us  [local(): jnp.where(inside, tall_grad * silu_slope(pre_one), 0.0).astype(jnp.bfloat16)]
    reshape x0 -> x2, local copies, waits for them, and re-layouts: none -> 1.19 us  [the longest x1 1.08 us: local(): maps[:, :, quads:].reshape(height2 // chunk, chunk * full2, filters)]
    broadcast_in_dim x1, local copies, waits for them, and re-layouts: 0.07 us -> 0.97 us  [local(): tall_grad = jnp.repeat(halves, 2, 0)[1:-1] * 0.25]
    slice x0 -> x2, local copies, waits for them, and re-layouts: none -> 0.85 us  [the longest x1 0.75 us: local(): maps[:, :, quads:].reshape(height2 // chunk, chunk * full2, filters)]
where the time goes in v4:
time: 60.6 us; the launch traced here: 60.2 us
  Pallas kernels  39 us (64%)
  local copies, waits for them, and re-layouts  14.1 us (23%)
  matrix products  3.16 us (5%)
  other arithmetic  2.82 us (5%)
  between operations  1.17 us (2%)
    pallas_call x1, Pallas kernels, first_layer(): pl.pallas_call(functools.partial(first_kernel, rows, strips), out_shape=(...  18.1 us
    pallas_call x1, Pallas kernels, last_layer(): pl.pallas_call(functools.partial(last_kernel, scale), out_shape=(jax.Shap...  12.2 us
    pallas_call x1, Pallas kernels, reduce_scatter(): pl.pallas_call(scatter_kernel, out_shape=(jax.ShapeDtypeStruct(blocks.sha...  8.7 us
    unnamed x24, local copies, waits for them, and re-layouts  8.37 us
    conv_general_dilated x3, matrix products, conv_valid(): lax.conv_general_dilated(cells[None], kernel, (1, 1), 'VALID', dimension_...  2.73 us
    convert_element_type x1, other arithmetic, local(): jnp.where(inside, tall_grad * silu_slope(pre_one), 0.0).astype(jnp.bfloat16)  1.76 us

profile of v4, /device:TPU:0, one launch (start us, length us, event | category | flops | bytes accessed | tf_op | source)
XLA Modules:
  0.0 60.2 jit_solution(12320824322569207222)
XLA Ops:
  0.6 0.0 copy-start
  0.7 0.1 and.120
  0.8 0.1 add.202
  0.9 0.1 add.203
  0.9 0.1 add.204
  1.0 0.1 fusion.29.pick_cols
  1.1 0.9 %copy.77 = bf16[128,32,8]{0,1,2:T(8,128)(2,1)S(1)} copy(bf16[128,32,8]{0,2,1:T(8,128)(2,1)} %param.7) | data formatting | bytes 131072 | tf_op args[3]
  2.0 1.0 %copy.41 = bf16[64,3,3,64]{0,3,2,1:T(8,128)(2,1)S(1)} copy(bf16[64,3,3,64]{3,0,2,1:T(8,128)(2,1)} %param.5) | data formatting | bytes 147456 | tf_op args[1]
  3.1 0.1 copy.42.kernel
  3.2 0.1 fusion.15.spread_lanes
  3.4 0.9 %copy.76 = bf16[64,8,128]{2,0,1:T(8,128)(2,1)S(1)} copy(bf16[64,8,128]{2,1,0:T(8,128)(2,1)} %param.4) | data formatting | bytes 262144 | tf_op args[0]
  4.3 18.1 %shard_map.67 = (bf16[2,16,128]{2,1,0:T(8,128)(2,1)S(1)}, f32[10,64,384]{2,1,0:T(8,128)S(1)}, bf16[4,80,256]{2,1,0:T(8,128)(2,1)S(1)}, bf16[12,192,384]{2,1,0:T(8,128)(2,1)S(1)}) custom-call(bf16[8,64,128]{2,1,0:T(8,128)(2,1)S(1)} %bitcast.91, bf16[2,16,128]{2,1,0:T(8,128)(2,1)S(1)} %pad_maximum_fusion.4.edge_up, bf16[64,576]{1,0:T(8,128)(2,1)S(1)} %copy.42.kernel, ...), custom_call_target="tpu_custom_call" | custom-call | tf_op jit(solution)/shard_map/pallas_call | solution.py:202
  22.4 0.0 copy-start.3
  22.4 0.0 copy-done
  22.5 1.2 %fusion.13 = f32[1,8,36,128]{3,0,2,1:T(1,128)S(1)} fusion(bf16[128,3,3,256]{3,0,2,1:T(8,128)(2,1)S(1)} %copy-done, bf16[1,10,38,256]{3,2,1,0:T(8,128)(2,1)S(1)} %pad_bitcast_fusion), kind=kOutput, calls=%fused_computation.22 | convolution fusion | flops 169869312 | bytes 931840 | tf_op jit(solution)/shard_map/conv_general_dilated | solution.py:498
  23.6 0.0 copy-done.3
  23.7 0.1 fusion.25
  23.8 1.0 %fusion.17 = bf16[1,8,34,256]{3,0,2,1:T(2,128)(2,1)S(1)} fusion(bf16[128,3,3,256]{3,0,2,1:T(8,128)(2,1)S(1)} %copy-done, bf16[1,10,36,128]{3,2,1,0:T(8,128)(2,1)S(1)} %pad_bitcast_fusion.1), kind=kOutput, calls=%fused_computation.33 | convolution fusion | flops 160432128 | bytes 821248 | tf_op jit(solution)/shard_map/conv_general_dilated | solution.py:498
  24.8 0.1 pad.22
  24.9 0.4 slice.69
  25.3 0.4 slice.70
  25.8 0.1 broadcast_in_dim.58
  25.9 0.1 copy.64
  26.0 0.3 fusion.6
  26.4 0.2 pad_maximum_fusion.1
  26.5 0.1 copy.50
  26.8 8.7 %shard_map.68 = (bf16[112,256]{1,0:T(8,128)(2,1)S(1)}, bf16[4,256,384]{2,1,0:T(8,128)(2,1)S(1)}) custom-call(bf16[4,112,256]{2,1,0:T(8,128)(2,1)S(1)} %pad.23.blocks, bf16[256,384]{1,0:T(8,128)(2,1)S(1)} %bitcast.88), custom_call_target="tpu_custom_call" | custom-call | tf_op jit(solution)/shard_map/pallas_call | solution.py:385
  35.5 0.2 convolution_convert_fusion
  35.7 0.2 reshape.273
  36.0 0.3 convolution_bitcast_fusion
  36.3 1.0 %broadcast_in_dim.61 = f32[6,2,64,130]{3,2,1,0:T(8,128)} broadcast(f32[6,64,130]{2,1,0:T(8,128)S(1)} %pad_maximum_fusion), dimensions={0,2,3} | broadcast | bytes 599040 | tf_op jit(solution)/shard_map/broadcast_in_dim | solution.py:558
  37.3 0.1 broadcast_and_fusion
  37.4 1.8 %fusion.4 = bf16[10,64,130]{2,1,0:T(8,128)(2,1)S(1)} fusion(f32[12,64,130]{2,1,0:T(8,128)} %bitcast.94, f32[10,64,384]{2,1,0:T(8,128)} %copy-done.3, pred[10,130]{1,0:T(8,128)(4,1)S(1)} %broadcast_and_fusion), kind=kLoop, calls=%fused_computation.11 | loop fusion | flops 915200 | bytes 833300 | tf_op jit(solution)/shard_map/convert_element_type | solution.py:564
  39.1 0.0 copy-start.4
  39.1 0.1 slice.100.gradient
  39.3 0.6 copy-done.4
  39.8 0.1 copy.57
  40.0 0.1 pad.24.whole
  40.1 0.7 %slice.101 = bf16[8,128,128]{2,1,0:T(8,128)(2,1)} slice(bf16[8,128,384]{2,1,0:T(8,128)(2,1)S(1)} %bitcast.93), slice={[0:8], [0:128], [256:384]} | slice | bytes 524288 | tf_op jit(solution)/shard_map/slice | solution.py:570
  40.9 1.1 %copy.58 = bf16[1,1024,128]{1,2,0:T(8,128)(2,1)S(1)} copy(bf16[1,1024,128]{2,1,0:T(8,128)(2,1)} %bitcast.97) | data formatting | bytes 524288 | tf_op jit(solution)/shard_map/reshape | solution.py:570
  42.0 12.2 %shard_map.69 = (bf16[4,16,576]{2,1,0:T(8,128)(2,1)S(1)}, f32[9,128,256]{2,1,0:T(8,128)S(1)}) custom-call(bf16[12,192,384]{2,1,0:T(8,128)(2,1)S(1)} %get-tuple-element.15.shifted, bf16[8,64,128]{2,1,0:T(8,128)(2,1)S(1)} %slice.100.gradient, bf16[1,128,1024]{2,1,0:T(8,128)(2,1)S(1)} %bitcast.86, bf16[10,130,256]{2,1,0:T(8,128)(2,1)S(1)} %pad.24.whole), custom_call_target="tpu_custom_call" | custom-call | tf_op jit(solution)/shard_map/pallas_call | solution.py:475
  54.2 0.0 copy-start.1
  54.2 1.0 %copy-done.1 = f32[9,128,256]{2,1,0:T(8,128)} copy-done((f32[9,128,256]{2,1,0:T(8,128)}, f32[9,128,256]{2,1,0:T(8,128)S(1)}, u32[]{:S(2)}) %copy-start.1) | copy-done | bytes 1179672
  55.2 0.0 copy-start.5
  55.2 0.2 mul.120
  55.4 0.7 %copy.60 = f32[64,3,3,64]{3,0,2,1:T(8,128)} copy(f32[64,3,3,64]{3,2,1,0:T(4,128)S(1)} %mul.120) | data formatting | bytes 294912
  56.1 0.0 copy-done.5
  56.1 0.3 copy.66
  56.4 0.0 copy-start.6
  56.4 0.0 copy-start.7
  56.4 0.1 pad.25.clone
  56.5 0.1 reshape.281
  56.7 0.6 %copy-done.6 = bf16[64,3,3,64]{3,0,2,1:T(8,128)(2,1)S(1)} copy-done((bf16[64,3,3,64]{3,0,2,1:T(8,128)(2,1)S(1)}, bf16[64,3,3,64]{3,0,2,1:T(8,128)(2,1)}, u32[]{:S(2)}) %copy-start.6) | copy-done | bytes 73752
  57.3 0.0 copy-done.7
  57.3 0.6 fusion
  57.9 0.0 copy-start.2
  58.0 0.9 %copy.59 = bf16[64,8,128]{2,1,0:T(8,128)(2,1)} copy(bf16[64,8,128]{0,1,2:T(8,128)(2,1)S(1)} %slice_bitcast_fusion) | data formatting | bytes 262144
  58.9 0.4 copy-done.2
  59.2 1.0 %copy.79 = f32[128,3,3,256]{3,0,2,1:T(8,128)} copy(f32[128,3,3,256]{3,0,2,1:T(8,128)S(1)} %bitcast.85) | data formatting | bytes 2359296
  (40 shorter events, 0.6 us)
Async XLA Ops:
  0.6 21.8 %copy-start = (bf16[128,3,3,256]{3,0,2,1:T(8,128)(2,1)S(1)}, bf16[128,3,3,256]{3,0,2,1:T(8,128)(2,1)}, u32[]{:S(2)}) copy-start(bf16[128,3,3,256]{3,0,2,1:T(8,128)(2,1)} %param.6) | copy-start | bytes 1769476
  22.4 1.2 %copy-start.3 = (f32[10,64,384]{2,1,0:T(8,128)}, f32[10,64,384]{2,1,0:T(8,128)S(1)}, u32[]{:S(2)}) copy-start(f32[10,64,384]{2,1,0:T(8,128)S(1)} %get-tuple-element.14) | copy-start | bytes 2949124
  39.1 0.7 %copy-start.4 = (bf16[10,64,130]{2,1,0:T(8,128)(2,1)}, bf16[10,64,130]{2,1,0:T(8,128)(2,1)S(1)}, u32[]{:S(2)}) copy-start(bf16[10,64,130]{2,1,0:T(8,128)(2,1)S(1)} %fusion.4) | copy-start | bytes 499204
  54.2 1.0 %copy-start.1 = (f32[9,128,256]{2,1,0:T(8,128)}, f32[9,128,256]{2,1,0:T(8,128)S(1)}, u32[]{:S(2)}) copy-start(f32[9,128,256]{2,1,0:T(8,128)S(1)} %get-tuple-element.18) | copy-start | bytes 3538948
  55.2 1.0 %copy-start.5 = (bf16[10,64,130]{2,1,0:T(8,128)(2,1)S(1)}, bf16[10,64,130]{2,1,0:T(8,128)(2,1)}, u32[]{:S(2)}) copy-start(bf16[10,64,130]{2,1,0:T(8,128)(2,1)} %copy-done.4) | copy-start | bytes 499204
  56.4 0.9 %copy-start.6 = (bf16[64,3,3,64]{3,0,2,1:T(8,128)(2,1)S(1)}, bf16[64,3,3,64]{3,0,2,1:T(8,128)(2,1)}, u32[]{:S(2)}) copy-start(bf16[64,3,3,64]{3,0,2,1:T(8,128)(2,1)} %param.5) | copy-start | bytes 221188
  56.4 0.9 %copy-start.7 = (pred[8,17]{0,1:T(8,128)(4,1)S(1)}, pred[8,17]{0,1:T(8,128)(4,1)}, u32[]{:S(2)}) copy-start(pred[8,17]{0,1:T(8,128)(4,1)} %constant.140) | copy-start | bytes 412
  57.9 1.3 %copy-start.2 = (f32[9,128,256]{2,1,0:T(8,128)S(1)}, f32[9,128,256]{2,1,0:T(8,128)}, u32[]{:S(2)}) copy-start(f32[9,128,256]{2,1,0:T(8,128)} %copy-done.1) | copy-start | bytes 3538948

commit v5 on v4

--- a/solution.py
+++ b/solution.py
@@ -23,8 +23,9 @@
 
 
 def params(number):
+    share = max(1, lax.axis_size("row") * lax.axis_size(STRIP) // 64)
     return pltpu.CompilerParams(
-        collective_id=number, has_side_effects=True, vmem_limit_bytes=40 * 1024 * 1024
+        collective_id=number, has_side_effects=True, vmem_limit_bytes=share * 12 * 1024 * 1024
     )
 
 
@@ -399,7 +400,7 @@
 
 
 def last_kernel(
-    scale, shifted, gradient, grad_two_in, whole, out, taps, blocks, landing, part, parts, mine, *semaphores
+    scale, shifted, gradient, maps, whole, out, taps, turned, blocks, landing, part, parts, mine, *semaphores
 ):
     rows, row, row_device = group("rows")
     strips, strip, strip_device = group("strips")
@@ -413,7 +414,7 @@
             barrier, inc=1, device_id=strip_device(lax.rem(strip + step, strips)), device_id_type=MESH
         )
     band, channels, width = gradient.shape
-    steps, _, spots = grad_two_in.shape
+    steps, filters, spots = turned.shape
     full2 = whole.shape[1] - 2
     chunk = spots // full2
     quads = whole.shape[2]
@@ -429,13 +430,17 @@
     for peer in range(strips):
         blocks[peer] = total[peer * height : (peer + 1) * height].astype(blocks.dtype)
 
+    for step in range(steps):
+        rows_of = maps[pl.ds(step * chunk, chunk), :, pl.ds(quads, filters)].reshape(spots, filters)
+        turned[step] = rows_of.astype(jnp.float32).T.astype(turned.dtype)
+
     def tap(index):
         first, second = divmod(index, 3)
 
         def product(step):
             window = whole[pl.ds(step * chunk + first, chunk), pl.ds(second, full2)]
             return scale * jnp.dot(
-                grad_two_in[step], window.reshape(spots, quads), preferred_element_type=jnp.float32
+                turned[step], window.reshape(spots, quads), preferred_element_type=jnp.float32
             )
 
         taps[index] = product(0)
@@ -467,20 +472,24 @@
     finish()
 
 
-def last_layer(shifted, gradient, grad_two_in, whole, scale, number):
+def last_layer(shifted, gradient, maps, whole, scale, number):
     rows, strips = group_size("rows"), group_size("strips")
     channels = gradient.shape[1]
     kind = jnp.bfloat16
+    height2, full2, depth = maps.shape
+    filters = depth - whole.shape[2]
+    chunk = max(1, 1024 // full2)
     piece = (channels // strips, 9 * channels)
     return pl.pallas_call(
         functools.partial(last_kernel, scale),
         out_shape=(
             jax.ShapeDtypeStruct((strips,) + piece, kind),
-            jax.ShapeDtypeStruct((9, grad_two_in.shape[1], whole.shape[2]), jnp.float32),
+            jax.ShapeDtypeStruct((9, filters, whole.shape[2]), jnp.float32),
         ),
         in_specs=[VMEM] * 4,
         out_specs=(VMEM,) * 2,
         scratch_shapes=[
+            pltpu.VMEM((height2 // chunk, filters, chunk * full2), kind),
             pltpu.VMEM((strips,) + piece, kind),
             pltpu.VMEM((strips,) + piece, kind),
             pltpu.VMEM(piece, kind),
@@ -491,7 +500,7 @@
         + sems(rows)
         + sems(strips),
         compiler_params=params(number),
-    )(shifted, gradient, grad_two_in, whole)
+    )(shifted, gradient, maps, whole)
 
 
 def conv_valid(cells, kernel, numbers):
@@ -566,12 +575,10 @@
     maps = jnp.transpose(maps.reshape(strips, height2, width2, quads + filters), (1, 0, 2, 3))
     maps = maps.reshape(height2, full2, quads + filters)
     whole = jnp.pad(maps[:, :, :quads], ((1, 1), (1, 1), (0, 0)))
-    chunk = max(1, 1024 // full2)
-    grad_two_in = maps[:, :, quads:].reshape(height2 // chunk, chunk * full2, filters)
     summed, taps = last_layer(
         shifted,
         grad_ext[1:-1, :, 1:-1],
-        jnp.transpose(grad_two_in, (0, 2, 1)),
+        maps,
         whole,
         1.0 / math.sqrt(height2 * full2),
         3,

time: 60.6 us -> 64.3 us (1.061)
  local copies, waits for them, and re-layouts: 14.1 us -> 19.1 us
  other arithmetic: 2.82 us -> 1.4 us
    unnamed x24, local copies, waits for them, and re-layouts: 8.37 us -> 11.5 us
    conv_general_dilated x4, local copies, waits for them, and re-layouts: 0.2 us -> 2.99 us  [conv_valid(): lax.conv_general_dilated(cells[None], kernel, (1, 1), 'VALID', dimension_...]
    broadcast_in_dim x3, local copies, waits for them, and re-layouts: 0.1 us -> 1.85 us  [conv_valid(): cells[None]]
    convert_element_type x1, other arithmetic: 1.76 us -> 0.35 us  [local(): jnp.where(inside, tall_grad * silu_slope(pre_one), 0.0).astype(jnp.bfloat16)]
    reshape x1 -> x0, local copies, waits for them, and re-layouts: 1.08 us -> none  [local(): maps[:, :, quads:].reshape(height2 // chunk, chunk * full2, filters)]
    broadcast_in_dim x1, local copies, waits for them, and re-layouts: 0.97 us -> 0.07 us  [local(): tall_grad = jnp.repeat(halves, 2, 0)[1:-1] * 0.25]
    slice x1 -> x0, local copies, waits for them, and re-layouts: 0.75 us -> none  [local(): maps[:, :, quads:].reshape(height2 // chunk, chunk * full2, filters)]
where the time goes in v5:
time: 64.3 us; the launch traced here: 63.9 us
  Pallas kernels  39.1 us (61%)
  local copies, waits for them, and re-layouts  19.1 us (30%)
  matrix products  3.16 us (5%)
  other arithmetic  1.4 us (2%)
  between operations  1.13 us (2%)
    pallas_call x1, Pallas kernels, first_layer(): pl.pallas_call(functools.partial(first_kernel, rows, strips), out_shape=(...  18.1 us
    pallas_call x1, Pallas kernels, last_layer(): pl.pallas_call(functools.partial(last_kernel, scale), out_shape=(jax.Shap...  12.3 us
    unnamed x24, local copies, waits for them, and re-layouts  11.5 us
    pallas_call x1, Pallas kernels, reduce_scatter(): pl.pallas_call(scatter_kernel, out_shape=(jax.ShapeDtypeStruct(blocks.sha...  8.7 us
    conv_general_dilated x4, local copies, waits for them, and re-layouts, conv_valid(): lax.conv_general_dilated(cells[None], kernel, (1, 1), 'VALID', dimension_...  2.99 us
    conv_general_dilated x3, matrix products, conv_valid(): lax.conv_general_dilated(cells[None], kernel, (1, 1), 'VALID', dimension_...  2.73 us
    broadcast_in_dim x3, local copies, waits for them, and re-layouts, conv_valid(): cells[None]  1.85 us

profile of v5, /device:TPU:0, one launch (start us, length us, event | category | flops | bytes accessed | tf_op | source)
XLA Modules:
  0.0 63.9 jit_solution(17028613743160455572)
XLA Ops:
  0.6 0.0 copy-start
  0.7 0.1 and.120
  0.8 0.1 add.202
  0.9 0.1 add.203
  1.0 0.1 add.204
  1.1 0.1 broadcast_and_fusion
  1.2 0.1 fusion.29.pick_cols
  1.3 0.9 %copy.74 = bf16[128,32,8]{0,1,2:T(8,128)(2,1)S(1)} copy(bf16[128,32,8]{0,2,1:T(8,128)(2,1)} %param.7) | data formatting | bytes 131072 | tf_op args[3]
  2.2 0.1 fusion.15.spread_lanes
  2.3 0.9 %copy.73 = bf16[64,8,128]{2,0,1:T(8,128)(2,1)S(1)} copy(bf16[64,8,128]{2,1,0:T(8,128)(2,1)} %param.4) | data formatting | bytes 262144 | tf_op args[0]
  3.2 1.0 %copy.39 = bf16[64,3,3,64]{0,3,2,1:T(8,128)(2,1)S(1)} copy(bf16[64,3,3,64]{3,0,2,1:T(8,128)(2,1)} %param.5) | data formatting | bytes 147456 | tf_op args[1]
  4.3 0.1 copy.40.kernel
  4.4 18.1 %shard_map.67 = (bf16[2,16,128]{2,1,0:T(8,128)(2,1)S(1)}, f32[10,64,384]{2,1,0:T(8,128)S(1)}, bf16[4,80,256]{2,1,0:T(8,128)(2,1)S(1)}, bf16[12,192,384]{2,1,0:T(8,128)(2,1)S(1)}) custom-call(bf16[8,64,128]{2,1,0:T(8,128)(2,1)S(1)} %bitcast.90, bf16[2,16,128]{2,1,0:T(8,128)(2,1)S(1)} %pad_maximum_fusion.4.edge_up, bf16[64,576]{1,0:T(8,128)(2,1)S(1)} %copy.40.kernel, ...), custom_call_target="tpu_custom_call" | custom-call | tf_op jit(solution)/shard_map/pallas_call | solution.py:203
  22.6 0.0 copy-start.3
  22.6 0.9 %copy-done.3 = f32[10,64,384]{2,1,0:T(8,128)} copy-done((f32[10,64,384]{2,1,0:T(8,128)}, f32[10,64,384]{2,1,0:T(8,128)S(1)}, u32[]{:S(2)}) %copy-start.3) | copy-done | bytes 983064
  23.6 0.0 copy-done
  23.6 1.2 %fusion.13 = f32[1,8,36,128]{3,0,2,1:T(1,128)S(1)} fusion(bf16[128,3,3,256]{3,0,2,1:T(8,128)(2,1)S(1)} %copy-done, bf16[1,10,38,256]{3,2,1,0:T(8,128)(2,1)S(1)} %pad_bitcast_fusion), kind=kOutput, calls=%fused_computation.22 | convolution fusion | flops 169869312 | bytes 931840 | tf_op jit(solution)/shard_map/conv_general_dilated | solution.py:507
  24.8 0.1 fusion.25
  24.9 1.0 %fusion.17 = bf16[1,8,34,256]{3,0,2,1:T(2,128)(2,1)S(1)} fusion(bf16[128,3,3,256]{3,0,2,1:T(8,128)(2,1)S(1)} %copy-done, bf16[1,10,36,128]{3,2,1,0:T(8,128)(2,1)S(1)} %pad_bitcast_fusion.1), kind=kOutput, calls=%fused_computation.33 | convolution fusion | flops 160432128 | bytes 821248 | tf_op jit(solution)/shard_map/conv_general_dilated | solution.py:507
  26.0 0.1 copy.61
  26.1 0.1 pad.22
  26.2 0.4 slice.67
  26.6 0.4 slice.66
  27.1 0.1 broadcast_in_dim.58
  27.2 0.3 fusion.6
  27.5 0.2 pad_maximum_fusion.1
  27.7 0.1 copy.48
  27.8 8.7 %shard_map.68 = (bf16[112,256]{1,0:T(8,128)(2,1)S(1)}, bf16[4,256,384]{2,1,0:T(8,128)(2,1)S(1)}) custom-call(bf16[4,112,256]{2,1,0:T(8,128)(2,1)S(1)} %pad.23.blocks, bf16[256,384]{1,0:T(8,128)(2,1)S(1)} %bitcast.87), custom_call_target="tpu_custom_call" | custom-call | tf_op jit(solution)/shard_map/pallas_call | solution.py:386
  36.5 0.2 convolution_convert_fusion
  36.7 0.1 copy.55
  36.8 0.2 reshape.270
  37.1 0.3 convolution_bitcast_fusion
  37.3 0.0 copy-start.4
  37.4 0.1 broadcast_in_dim.61
  37.5 1.0 %copy-done.4 = f32[10,64,384]{2,1,0:T(8,128)S(1)} copy-done((f32[10,64,384]{2,1,0:T(8,128)S(1)}, f32[10,64,384]{2,1,0:T(8,128)}, u32[]{:S(2)}) %copy-start.4) | copy-done | bytes 983064
  38.5 0.3 fusion.4
  38.9 0.0 copy-start.5
  38.9 0.7 %copy-done.5 = bf16[10,64,130]{2,1,0:T(8,128)(2,1)} copy-done((bf16[10,64,130]{2,1,0:T(8,128)(2,1)}, bf16[10,64,130]{2,1,0:T(8,128)(2,1)S(1)}, u32[]{:S(2)}) %copy-start.5) | copy-done | bytes 166424
  39.6 0.1 slice.96.gradient
  39.7 1.9 %copy.63 = bf16[64,10,1,130]{0,3,1,2:T(8,128)(2,1)} copy(bf16[64,10,1,130]{3,0,1,2:T(8,128)(2,1)} %bitcast.92) | data formatting | bytes 332800
  41.6 0.0 copy-start.6
  41.6 0.0 copy-start.7
  41.6 1.8 %pad.25.clone = bf16[64,10,1,136]{0,3,1,2:T(8,128)(2,1)} pad(bf16[64,10,1,130]{0,3,1,2:T(8,128)(2,1)} %copy.63, bf16[]{:T(256)} %constant.118.clone.1), padding=0_0x0_0x0_0x0_6 | pad | bytes 340482 | tf_op jit(solution)/shard_map/broadcast_in_dim | solution.py:508
  43.5 1.9 %reshape.277 = bf16[64,10,1,8,17]{0,4,3,1,2:T(8,128)(2,1)} reshape(bf16[64,10,1,136]{0,3,1,2:T(8,128)(2,1)} %pad.25.clone) | data formatting | bytes 348160 | tf_op jit(solution)/shard_map/conv_general_dilated | solution.py:507
  45.3 1.1 %copy.53 = bf16[64,10,1,8,17]{0,3,4,1,2:T(8,128)(2,1)S(1)} copy(bf16[64,10,1,8,17]{0,4,3,1,2:T(8,128)(2,1)} %reshape.277) | data formatting | bytes 348160 | tf_op jit(solution)/shard_map/conv_general_dilated | solution.py:507
  46.4 0.0 copy-done.6
  46.4 0.0 copy-done.7
  46.5 0.6 fusion
  47.1 0.9 %copy.56 = bf16[64,8,128]{2,1,0:T(8,128)(2,1)} copy(bf16[64,8,128]{0,1,2:T(8,128)(2,1)S(1)} %slice_bitcast_fusion) | data formatting | bytes 262144
  48.0 0.1 pad.24.whole
  48.2 12.3 %shard_map.69 = (bf16[4,16,576]{2,1,0:T(8,128)(2,1)S(1)}, f32[9,128,256]{2,1,0:T(8,128)S(1)}) custom-call(bf16[12,192,384]{2,1,0:T(8,128)(2,1)S(1)} %get-tuple-element.15.shifted, bf16[8,64,128]{2,1,0:T(8,128)(2,1)S(1)} %slice.96.gradient, bf16[8,128,384]{2,1,0:T(8,128)(2,1)S(1)} %bitcast.84, bf16[10,130,256]{2,1,0:T(8,128)(2,1)S(1)} %pad.24.whole), custom_call_target="tpu_custom_call" | custom-call | tf_op jit(solution)/shard_map/pallas_call | solution.py:483
  60.5 0.0 copy-start.1
  60.5 1.0 %copy-done.1 = f32[9,128,256]{2,1,0:T(8,128)} copy-done((f32[9,128,256]{2,1,0:T(8,128)}, f32[9,128,256]{2,1,0:T(8,128)S(1)}, u32[]{:S(2)}) %copy-start.1) | copy-done | bytes 1179672
  61.5 0.0 copy-start.2
  61.5 0.2 mul.120
  61.7 0.7 %copy.57 = f32[64,3,3,64]{3,0,2,1:T(8,128)} copy(f32[64,3,3,64]{3,2,1,0:T(4,128)S(1)} %mul.120) | data formatting | bytes 294912
  62.4 0.4 copy-done.2
  62.9 1.0 %copy.76 = f32[128,3,3,256]{3,0,2,1:T(8,128)} copy(f32[128,3,3,256]{3,0,2,1:T(8,128)S(1)} %bitcast.85) | data formatting | bytes 2359296
  (39 shorter events, 0.6 us)
Async XLA Ops:
  0.6 22.9 %copy-start = (bf16[128,3,3,256]{3,0,2,1:T(8,128)(2,1)S(1)}, bf16[128,3,3,256]{3,0,2,1:T(8,128)(2,1)}, u32[]{:S(2)}) copy-start(bf16[128,3,3,256]{3,0,2,1:T(8,128)(2,1)} %param.6) | copy-start | bytes 1769476
  22.6 0.9 %copy-start.3 = (f32[10,64,384]{2,1,0:T(8,128)}, f32[10,64,384]{2,1,0:T(8,128)S(1)}, u32[]{:S(2)}) copy-start(f32[10,64,384]{2,1,0:T(8,128)S(1)} %get-tuple-element.14) | copy-start | bytes 2949124
  37.3 1.2 %copy-start.4 = (f32[10,64,384]{2,1,0:T(8,128)S(1)}, f32[10,64,384]{2,1,0:T(8,128)}, u32[]{:S(2)}) copy-start(f32[10,64,384]{2,1,0:T(8,128)} %copy-done.3) | copy-start | bytes 2949124
  38.9 0.7 %copy-start.5 = (bf16[10,64,130]{2,1,0:T(8,128)(2,1)}, bf16[10,64,130]{2,1,0:T(8,128)(2,1)S(1)}, u32[]{:S(2)}) copy-start(bf16[10,64,130]{2,1,0:T(8,128)(2,1)S(1)} %fusion.4) | copy-start | bytes 499204
  41.6 4.8 %copy-start.6 = (bf16[64,3,3,64]{3,0,2,1:T(8,128)(2,1)S(1)}, bf16[64,3,3,64]{3,0,2,1:T(8,128)(2,1)}, u32[]{:S(2)}) copy-start(bf16[64,3,3,64]{3,0,2,1:T(8,128)(2,1)} %param.5) | copy-start | bytes 221188
  41.6 4.8 %copy-start.7 = (pred[8,17]{0,1:T(8,128)(4,1)S(1)}, pred[8,17]{0,1:T(8,128)(4,1)}, u32[]{:S(2)}) copy-start(pred[8,17]{0,1:T(8,128)(4,1)} %constant.140) | copy-start | bytes 412
  60.5 1.0 %copy-start.1 = (f32[9,128,256]{2,1,0:T(8,128)}, f32[9,128,256]{2,1,0:T(8,128)S(1)}, u32[]{:S(2)}) copy-start(f32[9,128,256]{2,1,0:T(8,128)S(1)} %get-tuple-element.18) | copy-start | bytes 3538948
  61.5 1.4 %copy-start.2 = (f32[9,128,256]{2,1,0:T(8,128)S(1)}, f32[9,128,256]{2,1,0:T(8,128)}, u32[]{:S(2)}) copy-start(f32[9,128,256]{2,1,0:T(8,128)} %copy-done.1) | copy-start | bytes 3538948

commit v6 on v5

--- a/solution.py
+++ b/solution.py
@@ -25,7 +25,7 @@
 def params(number):
     share = max(1, lax.axis_size("row") * lax.axis_size(STRIP) // 64)
     return pltpu.CompilerParams(
-        collective_id=number, has_side_effects=True, vmem_limit_bytes=share * 12 * 1024 * 1024
+        collective_id=number, has_side_effects=True, vmem_limit_bytes=share * 24 * 1024 * 1024
     )
 
 
@@ -583,6 +583,7 @@
         1.0 / math.sqrt(height2 * full2),
         3,
     )
+    grad_ext, summed = lax.optimization_barrier((grad_ext, summed))
     scale = 1.0 / math.sqrt(band * rows * width * strips)
     grad_one = summed.astype(jnp.float32).reshape(channels, 3, 3, channels) * scale
     grad_two = jnp.transpose(taps, (1, 0, 2)).reshape(filters, 3, 3, quads)

time: 64.3 us -> 57.1 us (0.89)
  local copies, waits for them, and re-layouts: 19.1 us -> 11.4 us
    unnamed x24, local copies, waits for them, and re-layouts: 11.5 us -> 8.42 us
    conv_general_dilated x4, local copies, waits for them, and re-layouts: 2.99 us -> 0.2 us  [conv_valid(): lax.conv_general_dilated(cells[None], kernel, (1, 1), 'VALID', dimension_...]
    broadcast_in_dim x3, local copies, waits for them, and re-layouts: 1.85 us -> 0.1 us  [conv_valid(): cells[None]]
where the time goes in v6:
time: 57.1 us; the launch traced here: 56.9 us
  Pallas kernels  39.1 us (68%)
  local copies, waits for them, and re-layouts  11.4 us (20%)
  matrix products  3.16 us (6%)
  other arithmetic  2 us (4%)
  between operations  1.17 us (2%)
    pallas_call x1, Pallas kernels, first_layer(): pl.pallas_call(functools.partial(first_kernel, rows, strips), out_shape=(...  18.1 us
    pallas_call x1, Pallas kernels, last_layer(): pl.pallas_call(functools.partial(last_kernel, scale), out_shape=(jax.Shap...  12.3 us
    pallas_call x1, Pallas kernels, reduce_scatter(): pl.pallas_call(scatter_kernel, out_shape=(jax.ShapeDtypeStruct(blocks.sha...  8.7 us
    unnamed x24, local copies, waits for them, and re-layouts  8.42 us
    conv_general_dilated x3, matrix products, conv_valid(): lax.conv_general_dilated(cells[None], kernel, (1, 1), 'VALID', dimension_...  2.73 us

profile of v6, /device:TPU:0, one launch (start us, length us, event | category | flops | bytes accessed | tf_op | source)
XLA Modules:
  0.0 56.9 jit_solution(3630584930057949752)
XLA Ops:
  0.6 0.0 copy-start
  0.7 0.1 and.120
  0.8 0.1 add.202
  0.9 0.1 add.203
  1.0 0.1 add.204
  1.1 0.7 %broadcast_and_fusion = pred[10,130]{1,0:T(8,128)(4,1)} fusion(pred[130]{0:T(512)(128)(4,1)S(1)} %compare_and_fusion.1, pred[10]{0:T(512)(128)(4,1)S(1)} %compare_and_fusion.2), kind=kLoop, calls=%fused_computation.65 | loop fusion | flops 1300 | bytes 1440 | tf_op jit(solution)/shard_map/and | solution.py:570
  1.8 0.1 fusion.29.pick_cols
  1.9 0.9 %copy.74 = bf16[128,32,8]{0,1,2:T(8,128)(2,1)S(1)} copy(bf16[128,32,8]{0,2,1:T(8,128)(2,1)} %param.7) | data formatting | bytes 131072 | tf_op args[3]
  2.8 0.1 fusion.15.spread_lanes
  2.9 0.9 %copy.73 = bf16[64,8,128]{2,0,1:T(8,128)(2,1)S(1)} copy(bf16[64,8,128]{2,1,0:T(8,128)(2,1)} %param.4) | data formatting | bytes 262144 | tf_op args[0]
  3.8 1.0 %copy.39 = bf16[64,3,3,64]{0,3,2,1:T(8,128)(2,1)S(1)} copy(bf16[64,3,3,64]{3,0,2,1:T(8,128)(2,1)} %param.5) | data formatting | bytes 147456 | tf_op args[1]
  4.9 0.1 copy.40.kernel
  5.0 18.1 %shard_map.67 = (bf16[2,16,128]{2,1,0:T(8,128)(2,1)S(1)}, f32[10,64,384]{2,1,0:T(8,128)S(1)}, bf16[4,80,256]{2,1,0:T(8,128)(2,1)S(1)}, bf16[12,192,384]{2,1,0:T(8,128)(2,1)S(1)}) custom-call(bf16[8,64,128]{2,1,0:T(8,128)(2,1)S(1)} %bitcast.90, bf16[2,16,128]{2,1,0:T(8,128)(2,1)S(1)} %pad_maximum_fusion.4.edge_up, bf16[64,576]{1,0:T(8,128)(2,1)S(1)} %copy.40.kernel, ...), custom_call_target="tpu_custom_call" | custom-call | tf_op jit(solution)/shard_map/pallas_call | solution.py:203
  23.1 0.0 copy-start.3
  23.2 0.0 copy-done
  23.2 1.2 %fusion.13 = f32[1,8,36,128]{3,0,2,1:T(1,128)S(1)} fusion(bf16[128,3,3,256]{3,0,2,1:T(8,128)(2,1)S(1)} %copy-done, bf16[1,10,38,256]{3,2,1,0:T(8,128)(2,1)S(1)} %pad_bitcast_fusion), kind=kOutput, calls=%fused_computation.22 | convolution fusion | flops 169869312 | bytes 931840 | tf_op jit(solution)/shard_map/conv_general_dilated | solution.py:507
  24.4 0.0 copy-done.3
  24.4 0.1 fusion.25
  24.6 1.0 %fusion.17 = bf16[1,8,34,256]{3,0,2,1:T(2,128)(2,1)S(1)} fusion(bf16[128,3,3,256]{3,0,2,1:T(8,128)(2,1)S(1)} %copy-done, bf16[1,10,36,128]{3,2,1,0:T(8,128)(2,1)S(1)} %pad_bitcast_fusion.1), kind=kOutput, calls=%fused_computation.33 | convolution fusion | flops 160432128 | bytes 821248 | tf_op jit(solution)/shard_map/conv_general_dilated | solution.py:507
  25.7 0.1 copy.61
  25.8 0.1 pad.22
  25.9 0.4 slice.67
  26.3 0.4 slice.66
  26.8 0.1 broadcast_in_dim.58
  26.9 0.3 fusion.6
  27.2 0.2 pad_maximum_fusion.1
  27.4 0.1 copy.48
  27.5 8.7 %shard_map.68 = (bf16[112,256]{1,0:T(8,128)(2,1)S(1)}, bf16[4,256,384]{2,1,0:T(8,128)(2,1)S(1)}) custom-call(bf16[4,112,256]{2,1,0:T(8,128)(2,1)S(1)} %pad.23.blocks, bf16[256,384]{1,0:T(8,128)(2,1)S(1)} %bitcast.87), custom_call_target="tpu_custom_call" | custom-call | tf_op jit(solution)/shard_map/pallas_call | solution.py:386
  36.2 0.2 convolution_convert_fusion
  36.4 0.1 copy.51
  36.5 0.2 reshape.270
  36.7 0.3 convolution_bitcast_fusion
  37.0 0.0 copy-start.4
  37.0 0.0 copy-start.6
  37.1 0.1 broadcast_in_dim.61
  37.2 1.0 %copy-done.4 = f32[10,64,384]{2,1,0:T(8,128)S(1)} copy-done((f32[10,64,384]{2,1,0:T(8,128)S(1)}, f32[10,64,384]{2,1,0:T(8,128)}, u32[]{:S(2)}) %copy-start.4) | copy-done | bytes 983064
  38.2 0.0 copy-done.6
  38.2 0.3 fusion.4
  38.6 0.1 slice.94.gradient
  38.7 0.1 pad.24.whole
  38.9 12.3 %shard_map.69 = (bf16[4,16,576]{2,1,0:T(8,128)(2,1)S(1)}, f32[9,128,256]{2,1,0:T(8,128)S(1)}) custom-call(bf16[12,192,384]{2,1,0:T(8,128)(2,1)S(1)} %get-tuple-element.17.shifted, bf16[8,64,128]{2,1,0:T(8,128)(2,1)S(1)} %slice.94.gradient, bf16[8,128,384]{2,1,0:T(8,128)(2,1)S(1)} %bitcast.84, bf16[10,130,256]{2,1,0:T(8,128)(2,1)S(1)} %pad.24.whole), custom_call_target="tpu_custom_call" | custom-call | tf_op jit(solution)/shard_map/pallas_call | solution.py:483
  51.2 0.0 copy-start.1
  51.2 1.0 %copy-done.1 = f32[9,128,256]{2,1,0:T(8,128)} copy-done((f32[9,128,256]{2,1,0:T(8,128)}, f32[9,128,256]{2,1,0:T(8,128)S(1)}, u32[]{:S(2)}) %copy-start.1) | copy-done | bytes 1179672
  52.2 0.3 copy.63
  52.4 0.0 copy-start.5
  52.5 0.0 copy-start.7
  52.5 0.1 pad.25.clone
  52.5 0.1 reshape.277
  52.8 0.6 %copy-done.5 = bf16[64,3,3,64]{3,0,2,1:T(8,128)(2,1)S(1)} copy-done((bf16[64,3,3,64]{3,0,2,1:T(8,128)(2,1)S(1)}, bf16[64,3,3,64]{3,0,2,1:T(8,128)(2,1)}, u32[]{:S(2)}) %copy-start.5) | copy-done | bytes 73752
  53.4 0.0 copy-done.7
  53.4 0.6 %fusion = bf16[8,8,17,64]{3,1,2,0:T(8,128)(2,1)S(1)} fusion(bf16[64,3,3,64]{3,0,2,1:T(8,128)(2,1)S(1)} %copy-done.5, bf16[64,10,1,7,2]{0,3,4,1,2:T(8,128)(2,1)S(1)} %slice.96, bf16[64,10,1,8,17]{0,3,4,1,2:T(8,128)(2,1)S(1)} %copy.54, pred[8,17]{0,1:T(8,128)(4,1)S(1)} %copy-done.7), kind=kOutput, calls=%fused_computation.1 | convolution fusion | flops 80939008 | bytes 405128 | tf_op jit(solution)/shard_map/conv_general_dilated | solution.py:507
  54.0 0.0 copy-start.2
  54.0 0.9 %copy.56 = bf16[64,8,128]{2,1,0:T(8,128)(2,1)} copy(bf16[64,8,128]{0,1,2:T(8,128)(2,1)S(1)} %slice_bitcast_fusion) | data formatting | bytes 262144
  54.9 0.2 mul.120
  55.1 0.7 %copy.57 = f32[64,3,3,64]{3,0,2,1:T(8,128)} copy(f32[64,3,3,64]{3,2,1,0:T(4,128)S(1)} %mul.120) | data formatting | bytes 294912
  55.8 0.0 copy-done.2
  55.8 1.0 %copy.76 = f32[128,3,3,256]{3,0,2,1:T(8,128)} copy(f32[128,3,3,256]{3,0,2,1:T(8,128)S(1)} %bitcast.85) | data formatting | bytes 2359296
  (40 shorter events, 0.6 us)
Async XLA Ops:
  0.6 22.6 %copy-start = (bf16[128,3,3,256]{3,0,2,1:T(8,128)(2,1)S(1)}, bf16[128,3,3,256]{3,0,2,1:T(8,128)(2,1)}, u32[]{:S(2)}) copy-start(bf16[128,3,3,256]{3,0,2,1:T(8,128)(2,1)} %param.6) | copy-start | bytes 1769476
  23.1 1.3 %copy-start.3 = (f32[10,64,384]{2,1,0:T(8,128)}, f32[10,64,384]{2,1,0:T(8,128)S(1)}, u32[]{:S(2)}) copy-start(f32[10,64,384]{2,1,0:T(8,128)S(1)} %get-tuple-element.16) | copy-start | bytes 2949124
  37.0 1.2 %copy-start.4 = (f32[10,64,384]{2,1,0:T(8,128)S(1)}, f32[10,64,384]{2,1,0:T(8,128)}, u32[]{:S(2)}) copy-start(f32[10,64,384]{2,1,0:T(8,128)} %copy-done.3) | copy-start | bytes 2949124
  37.0 1.2 %copy-start.6 = (pred[10,130]{1,0:T(8,128)(4,1)S(1)}, pred[10,130]{1,0:T(8,128)(4,1)}, u32[]{:S(2)}) copy-start(pred[10,130]{1,0:T(8,128)(4,1)} %broadcast_and_fusion) | copy-start | bytes 3904
  51.2 1.0 %copy-start.1 = (f32[9,128,256]{2,1,0:T(8,128)}, f32[9,128,256]{2,1,0:T(8,128)S(1)}, u32[]{:S(2)}) copy-start(f32[9,128,256]{2,1,0:T(8,128)S(1)} %get-tuple-element.22) | copy-start | bytes 3538948
  52.4 0.9 %copy-start.5 = (bf16[64,3,3,64]{3,0,2,1:T(8,128)(2,1)S(1)}, bf16[64,3,3,64]{3,0,2,1:T(8,128)(2,1)}, u32[]{:S(2)}) copy-start(bf16[64,3,3,64]{3,0,2,1:T(8,128)(2,1)} %param.5) | copy-start | bytes 221188
  52.5 0.9 %copy-start.7 = (pred[8,17]{0,1:T(8,128)(4,1)S(1)}, pred[8,17]{0,1:T(8,128)(4,1)}, u32[]{:S(2)}) copy-start(pred[8,17]{0,1:T(8,128)(4,1)} %constant.140) | copy-start | bytes 412
  54.0 1.8 %copy-start.2 = (f32[9,128,256]{2,1,0:T(8,128)S(1)}, f32[9,128,256]{2,1,0:T(8,128)}, u32[]{:S(2)}) copy-start(f32[9,128,256]{2,1,0:T(8,128)} %copy-done.1) | copy-start | bytes 3538948
